TPU v7x, 32 devices: a whole 2x2x4 slice. The times are simulated.
32 devices in a mesh: dp: 8 (over z, y), head: 4 (over x, core).
Axes of the slice: x: 2, y: 2, z: 4, core: 2. Of those that a mesh axis runs over, the one named last changes fastest.
Arguments:
- tokens: bfloat16 [16384, 768], P(('dp', 'head')), may hold values from -6 to 6
- seq_len: int32 [128], P('dp'), may hold values from 128 to 512, as said below
- norm1_gain: float32 [768], replicated, may hold values from 0.25 to 1.75
- norm1_bias: float32 [768], replicated, may hold values from -1.75 to 1.75
- f1_weight: bfloat16 [12, 768, 768], P('head'), may hold values from -0.21875 to 0.21875
- f1_bias: float32 [12, 768], P('head'), may hold values from -3 to 3
- f2_weight: bfloat16 [12, 768, 512], P('head'), may hold values from -0.4375 to 0.4375
- f2_bias: float32 [12, 512], P('head'), may hold values from -3 to 3
- value_weight: bfloat16 [768, 768], P(None, 'head'), may hold values from -0.21875 to 0.21875
- out_weight: bfloat16 [768, 768], replicated, may hold values from -0.875 to 0.875
- norm2_gain: float32 [768], replicated, may hold values from 0.25 to 1.75
- norm2_bias: float32 [768], replicated, may hold values from -1.75 to 1.75
- up_weight: bfloat16 [768, 3072], P(None, 'head'), may hold values from -0.21875 to 0.21875
- up_bias: float32 [3072], P('head'), may hold values from -3 to 3
- down_weight: bfloat16 [3072, 768], P('head'), may hold values from -0.109375 to 0.109375
- down_bias: float32 [768], replicated, may hold values from -1.75 to 1.75
- out_grad: bfloat16 [16384, 768], P(('dp', 'head')), may hold values from -6 to 6
Outputs:
- result: float32 [16384, 768], P(('dp', 'head'))
- input_grad: float32 [16384, 768], P(('dp', 'head'))
- norm1_gain_grad: float32 [768], replicated
- norm1_bias_grad: float32 [768], replicated
- f1_weight_grad: float32 [12, 768, 768], P('head', 'dp')
- f1_bias_grad: float32 [12, 768], replicated
- f2_weight_grad: float32 [12, 768, 512], P('head', 'dp')
- f2_bias_grad: float32 [12, 512], replicated
- value_weight_grad: float32 [768, 768], P('dp', 'head')
- out_weight_grad: float32 [768, 768], P('dp')
- norm2_gain_grad: float32 [768], replicated
- norm2_bias_grad: float32 [768], replicated
- up_weight_grad: float32 [768, 3072], P('dp', 'head')
- up_bias_grad: float32 [3072], replicated
- down_weight_grad: float32 [3072, 768], P('head', 'dp')
- down_bias_grad: float32 [768], replicated
Inputs may be any that keep to these rules, and one draw needn't show every extreme that they name: `seq_len`: each aligned block of 512 rows is cut into sequences of 128, 256 or 512 rows, each starting at a multiple of its own length; every row of a sequence has its length.
All inputs are finite; a program needn't handle non-finite values.
Results may differ from a plain program's by a relative error of at most 0.017.
Values may be sent and summed in bfloat16 or wider, within the bound.
A program may use at most 256 MiB of HBM per device.

v0:
```python
import types

import jax
import jax.numpy as jnp
from jax import lax
from jax.experimental import pallas as pl
from jax.experimental.pallas import tpu as pltpu
from jax.sharding import PartitionSpec as P

F32 = jnp.float32
BF16 = jnp.bfloat16
BLOCK = 128
VMEM_LIMIT = 50 << 20
FUSED_LIMIT = 62 << 20


def mm(a, b):
    return lax.dot_general(a, b, (((1,), (0,)), ((), ())), preferred_element_type=F32)


def mm_nt(a, b):
    return lax.dot_general(a, b, (((1,), (1,)), ((), ())), preferred_element_type=F32)


def mm_tn(a, b):
    return lax.dot_general(a, b, (((0,), (0,)), ((), ())), preferred_element_type=F32)


def standardize(values):
    centred = values - jnp.mean(values, -1, keepdims=True)
    inv_std = lax.rsqrt(jnp.mean(centred * centred, -1, keepdims=True) + 1e-05)
    return centred * inv_std, inv_std


def norm_back(grad_out, scaled, inv_std, gain):
    grad_scaled = grad_out * gain
    centre_mean = jnp.mean(grad_scaled, -1, keepdims=True)
    cross_mean = jnp.mean(grad_scaled * scaled, -1, keepdims=True)
    return inv_std * (grad_scaled - centre_mean - scaled * cross_mean)


def silu_and_slope(pre_val):
    sigma = 0.5 + 0.5 * jnp.tanh(0.5 * pre_val)
    gated = pre_val * sigma
    return gated, sigma + gated * (1.0 - sigma)


def add_low(a, b):
    return (a.astype(F32) + b.astype(F32)).astype(BF16)


def swap(value, axis, step):
    return lax.ppermute(value, axis, [(i, i ^ step) for i in range(lax.axis_size(axis))])


def cost(macs, bytes_accessed):
    return pl.CostEstimate(flops=2 * macs, bytes_accessed=bytes_accessed, transcendentals=0)


def store_shards(keep_ref, send_ref, lanes, acc_ref):
    count, depth = keep_ref.shape[:2]
    me = lax.axis_index("dp")
    pair, parity = me // 2, me % 2
    for k in range(count):
        other = jnp.bitwise_xor(pair, k) * 2
        mine = pl.multiple_of((other + parity) * depth, 8)
        theirs = pl.multiple_of((other + 1 - parity) * depth, 8)
        keep_ref[k, :, lanes] = acc_ref[pl.ds(mine, depth), :].astype(BF16)
        send_ref[k, :, lanes] = acc_ref[pl.ds(theirs, depth), :].astype(BF16)


def shard_shape(width, lanes):
    members = lax.axis_size("dp")
    return jax.ShapeDtypeStruct((members // 2, width // members, lanes), BF16)


class Wires:
    def __init__(self, send, recv):
        self.send, self.recv, self.used = send, recv, 0
        self.all = []

    def remote(self, src, dst, axis, step):
        index = self.used
        self.used += 1
        move = pltpu.make_async_remote_copy(
            src_ref=src,
            dst_ref=dst,
            send_sem=self.send.at[index],
            recv_sem=self.recv.at[index],
            device_id={axis: jnp.bitwise_xor(lax.axis_index(axis), step)},
            device_id_type=pl.DeviceIdType.MESH,
        )
        self.all.append(move)
        return move


class Shards:
    def __init__(self, wires, keep, send, got, out, local_sem):
        self.keep, self.got, self.out = keep, got, out
        self.count = keep.shape[0]
        self.first = wires.remote(send, got, "dp", 1)
        self.rest = [
            wires.remote(keep.at[k], out.at[k], "dp", 2 * k) for k in range(1, self.count)
        ]
        self.own = pltpu.make_async_copy(keep.at[0], out.at[0], local_sem)

    def start(self):
        self.first.start()

    def second(self):
        self.first.wait_recv()
        for k in list(range(1, self.count)) + [0]:
            self.keep[k] = add_low(self.keep[k], self.got[k])
            (self.rest[k - 1] if k else self.own).start()

    def finish(self):
        for move in self.rest:
            move.wait_recv()
        self.own.wait()


def greet(axes):
    barrier = pltpu.get_barrier_semaphore()
    for axis, step in axes:
        pl.semaphore_signal(
            barrier,
            1,
            device_id={axis: jnp.bitwise_xor(lax.axis_index(axis), step)},
            device_id_type=pl.DeviceIdType.MESH,
        )
    pl.semaphore_wait(barrier, len(axes))


def partners():
    over_dp = [1] + list(range(2, lax.axis_size("dp"), 2))
    return [("head", s) for s in range(1, lax.axis_size("head"))] + [("dp", s) for s in over_dp]


FRONT_IN = (
    "lens", "x", "og", "vecs", "f1b", "f2b", "vt", "f1", "f2",
    "ow", "up", "down",
)
FRONT_OUT = (
    "xs_o", "n1t_o", "hid_o", "slope_o", "prob_o", "valt_o", "mgt_o", "f_o", "rg_o", "res_o",
    "down_o", "up_o", "okeep_o", "osend_o", "upb_sum", "sums",
)
FRONT_SCRATCH = (
    "xs", "n1", "n1t", "f1v", "f2v", "hidb", "slopeb", "probb", "valt", "mixt", "attt", "owv",
    "upv", "downv", "ogs", "n2s", "act", "pug", "near1", "near3", "crossb", "crossr",
    "fterms", "res", "low", "mgt", "mgts", "acc", "dkeep", "dsend", "dgot", "ukeep", "usend", "ugot", "okeep", "osend", "send",
    "recv", "load", "spill", "store",
)


def split_prob(parts, length, longest, b, zero):
    is_full = length == longest
    is_half = length == longest // 2
    for c in range(len(parts)):
        half = parts[c % 2] if c // 2 == b // 2 else zero
        quarter = parts[0] if c == b else zero
        yield c, jnp.where(is_full, parts[c], jnp.where(is_half, half, quarter))


def cells(row):
    return [row[:, c : c + BLOCK] for c in range(0, row.shape[1], BLOCK)]


def front_kernel(*refs):
    r = types.SimpleNamespace(**dict(zip(FRONT_IN + FRONT_OUT + FRONT_SCRATCH, refs)))
    r.terms = r.xs
    slabs, rows, width = r.xs.shape
    heads, _, longest = r.f2v.shape
    depth = r.mixt.shape[1]
    dim = depth // heads
    half = rows // 2
    blocks = rows // BLOCK
    me = lax.axis_index("head")

    w = Wires(r.send, r.recv)
    down_group = Shards(w, r.dkeep, r.dsend, r.dgot, r.down_o, r.store.at[3])
    up_group = Shards(w, r.ukeep, r.usend, r.ugot, r.up_o, r.store.at[4])

    def remote(src, dst, step):
        return w.remote(src, dst, "head", step)

    def cut(c):
        return pl.ds(c * half, half)

    my_rows = pl.ds(pl.multiple_of(me * depth, depth), depth)
    moves = {
        "x1": remote(r.x, r.xs.at[1], 1),
        "x2": remote(r.x, r.xs.at[2], 2),
        "x3": remote(r.xs.at[2], r.xs.at[3], 1),
        "o1": remote(r.og, r.ogs.at[1], 1),
        "o2": remote(r.og, r.ogs.at[2], 2),
        "o3": remote(r.ogs.at[2], r.ogs.at[3], 1),
        "t1": remote(r.terms.at[1], r.near1, 1),
    }
    for j in range(1, slabs):
        moves[f"m{j}"] = remote(r.mixt.at[j], r.attt.at[my_rows], j)
        piece = pl.ds(pl.multiple_of(jnp.bitwise_xor(me, j) * depth, depth), depth)
        moves[f"g{j}"] = remote(r.mgt.at[piece], r.mgts.at[j], j)
    for c in range(2):
        part = cut(c)
        moves[f"n1{c}"] = remote(r.n2s.at[0, part], r.n2s.at[1, part], 1)
        moves[f"n2{c}"] = remote(r.n2s.at[0, part], r.n2s.at[2, part], 2)
        moves[f"n3{c}"] = remote(r.n2s.at[2, part], r.n2s.at[3, part], 1)
        moves[f"t3{c}"] = remote(r.terms.at[3, part], r.near3.at[part], 1)
        moves[f"c{c}"] = remote(r.crossb.at[part], r.crossr.at[part], 2)

    loads = [pltpu.make_async_copy(r.x, r.xs.at[0], r.load.at[0])]
    for h in range(heads):
        loads.append(pltpu.make_async_copy(r.f1.at[h], r.f1v.at[h], r.load.at[1 + 2 * h]))
        loads.append(pltpu.make_async_copy(r.f2.at[h], r.f2v.at[h], r.load.at[2 + 2 * h]))
    base = 1 + 2 * heads
    late = [
        pltpu.make_async_copy(r.ow, r.owv, r.load.at[base]),
        pltpu.make_async_copy(r.up, r.upv, r.load.at[base + 1]),
        pltpu.make_async_copy(r.down, r.downv, r.load.at[base + 2]),
        pltpu.make_async_copy(r.og, r.ogs.at[0], r.load.at[base + 3]),
    ]
    for copy in loads:
        copy.start()
    greet(partners())
    moves["x2"].start()
    moves["x1"].start()
    for copy in late:
        copy.start()
    loads[0].wait()

    def spills(j, h, slot):
        return [
            pltpu.make_async_copy(r.hidb.at[slot], r.hid_o.at[j, h], r.spill.at[slot, 0]),
            pltpu.make_async_copy(r.slopeb.at[slot], r.slope_o.at[j, h], r.spill.at[slot, 1]),
            pltpu.make_async_copy(r.probb.at[slot], r.prob_o.at[j, h], r.spill.at[slot, 2]),
        ]

    def slab_step(j, carry):
        @pl.when(j == 1)
        def _():
            moves["x1"].wait_recv()

        @pl.when(j == 2)
        def _():
            moves["x2"].wait_recv()
            moves["x3"].start()
            moves["o2"].start()
            moves["o1"].start()

        @pl.when(j == 3)
        def _():
            moves["x3"].wait_recv()

        scaled, _ = standardize(r.xs[j].astype(F32))
        low = (scaled * r.vecs[0:1] + r.vecs[1:2]).astype(BF16)
        r.n1[...] = low
        r.n1t[j] = low.T
        r.valt[j] = mm(r.vt[...], r.n1t[j]).astype(BF16)

        def head_step(h, carry):
            turn = j * heads + h
            slot = turn % 2

            @pl.when(j == 0)
            def _():
                pltpu.make_async_copy(r.f1.at[h], r.f1v.at[h], r.load.at[1 + 2 * h]).wait()
                pltpu.make_async_copy(r.f2.at[h], r.f2v.at[h], r.load.at[2 + 2 * h]).wait()

            @pl.when(turn >= 2)
            def _():
                for copy in spills(j, h, slot):
                    copy.wait()

            first = jnp.bitwise_xor(me, j) * blocks
            column = lax.broadcasted_iota(jnp.int32, (BLOCK, longest), 1)
            zero = jnp.zeros((BLOCK, BLOCK), F32)
            for c in range(2):
                part = slice(c * half, (c + 1) * half)
                gated, slope = silu_and_slope(mm(r.n1[part], r.f1v[h]) + r.f1b[pl.ds(h, 1)])
                hidden = gated.astype(BF16)
                r.hidb[slot, part] = hidden
                r.slopeb[slot, part] = slope.astype(BF16)
                scores = mm(hidden, r.f2v[h]) + r.f2b[pl.ds(h, 1)]
                for i in range(half // BLOCK):
                    b = c * (half // BLOCK) + i
                    length = r.lens[first + b]
                    own = scores[i * BLOCK : (i + 1) * BLOCK]
                    keep = column < length
                    top = jnp.max(jnp.where(keep, own, -3.0e38), -1, keepdims=True)
                    exp_val = jnp.where(keep, jnp.exp(own - top), 0.0)
                    prob = exp_val * (1.0 / jnp.sum(exp_val, -1, keepdims=True))
                    for k, cell in split_prob(cells(prob), length, longest, b, zero):
                        r.probb[
                            slot, b * BLOCK : (b + 1) * BLOCK, k * BLOCK : (k + 1) * BLOCK
                        ] = cell.astype(BF16)
            own_rows = pl.ds(pl.multiple_of(h * dim, dim), dim)
            r.mixt[j, own_rows] = mm_nt(r.valt[j, own_rows], r.probb[slot]).astype(BF16)
            for copy in spills(j, h, slot):
                copy.start()
            return carry

        lax.fori_loop(0, heads, head_step, 0)
        for k in range(1, slabs):

            @pl.when(j == k)
            def _(k=k):
                moves[f"m{k}"].start()

        return carry

    lax.fori_loop(0, slabs, slab_step, 0)
    stores = [
        pltpu.make_async_copy(r.xs, r.xs_o, r.store.at[0]),
        pltpu.make_async_copy(r.n1t, r.n1t_o, r.store.at[1]),
        pltpu.make_async_copy(r.valt, r.valt_o, r.store.at[2]),
    ]
    for copy in stores:
        copy.start()
    r.attt[my_rows] = r.mixt[0]
    moves["o2"].wait_recv()
    moves["o3"].start()
    for copy in late:
        copy.wait()
    for j in range(1, slabs):
        moves[f"m{j}"].wait_recv()

    for c in range(2):
        part = slice(c * half, (c + 1) * half)
        residual = r.xs[0, part].astype(F32) + mm_tn(r.attt[:, part], r.owv[...])
        r.res[part] = residual
        scaled, _ = standardize(residual)
        r.n2s[0, part] = (scaled * r.vecs[2:3] + r.vecs[3:4]).astype(BF16)
        moves[f"n2{c}"].start()
        moves[f"n1{c}"].start()

    stores.pop(0).wait()
    sent = moves["x3"]
    sent.wait_send()

    def ffn_step(u, carry):
        v = u - 4
        j = jnp.where(u < 4, u // 2, 2 + v % 2)
        c = jnp.where(u < 4, u % 2, v // 2)

        @pl.when(u == 2)
        def _():
            moves["n10"].wait_recv()
            moves["o1"].wait_recv()

        @pl.when(u == 3)
        def _():
            moves["n11"].wait_recv()

        @pl.when(u == 4)
        def _():
            moves["n20"].wait_recv()
            moves["n30"].start()

        @pl.when(u == 5)
        def _():
            moves["o3"].wait_recv()
            moves["n30"].wait_recv()

        @pl.when(u == 6)
        def _():
            moves["n21"].wait_recv()
            moves["n31"].start()

        @pl.when(u == 7)
        def _():
            moves["n31"].wait_recv()

        part = pl.ds(pl.multiple_of(c * half, half), half)
        gated, slope = silu_and_slope(mm(r.n2s[j, part], r.upv[...]) + r.vecs[4:5])
        act = gated.astype(BF16)
        r.act[j, part] = act
        pug = (mm_nt(r.ogs[j, part], r.downv[...]) * slope).astype(BF16)
        r.pug[j, part] = pug
        r.terms[j, part] = mm_nt(pug, r.upv[...]).astype(BF16)
        r.fterms[j, part] = mm(act, r.downv[...]).astype(BF16)

        @pl.when(u == 3)
        def _():
            moves["t1"].start()

        @pl.when(u == 5)
        def _():
            moves["t30"].start()

        @pl.when(u == 6)
        def _():
            moves["t30"].wait_recv()
            r.crossb[0:half] = add_low(r.terms[2, 0:half], r.near3[0:half])
            moves["c0"].start()

        @pl.when(u == 7)
        def _():
            moves["t31"].start()

        return carry

    lax.fori_loop(0, 8, ffn_step, 0)
    flat = (slabs * rows, width)
    units = r.act.shape[2]
    r.upb_sum[...] = jnp.sum(r.pug[...].reshape(flat).astype(F32), 0, keepdims=True)
    moves["t31"].wait_recv()
    r.crossb[half:] = add_low(r.terms[2, half:], r.near3[half:])
    moves["c1"].start()
    r.acc[...] = mm_tn(r.ogs[...].reshape(flat), r.act[...].reshape(flat))
    store_shards(r.dkeep, r.dsend, slice(None), r.acc)
    down_group.start()
    r.acc[...] = mm_tn(r.n2s[...].reshape(flat), r.pug[...].reshape(flat))
    store_shards(r.ukeep, r.usend, slice(None), r.acc)
    up_group.start()
    more = [
        pltpu.make_async_copy(r.fterms, r.f_o, r.store.at[5]),
        pltpu.make_async_copy(r.res, r.res_o, r.store.at[6]),
    ]
    for copy in more:
        copy.start()
    stores += more
    cot = r.ogs[0].astype(F32)
    r.sums[2:3] = jnp.sum(cot, 0, keepdims=True)
    moves["t1"].wait_recv()
    moves["c0"].wait_recv()
    moves["c1"].wait_recv()

    grad = r.terms[0].astype(F32) + r.near1[...].astype(F32) + r.crossr[...].astype(F32)
    scaled, inv_std = standardize(r.res[...])
    res_grad = cot + norm_back(grad, scaled, inv_std, r.vecs[2:3])
    r.rg_o[...] = res_grad
    r.low[...] = res_grad.astype(BF16)
    r.sums[0:1] = jnp.sum(grad * scaled, 0, keepdims=True)
    r.sums[1:2] = jnp.sum(grad, 0, keepdims=True)
    r.mgt[...] = mm_nt(r.owv[...], r.low[...]).astype(BF16)
    for j in (2, 3, 1):
        moves[f"g{j}"].start()
    down_group.second()
    r.mgts[0] = r.mgt[my_rows]
    r.acc[...] = mm(r.attt[...], r.low[...])
    store_shards(r.okeep, r.osend, slice(None), r.acc)
    more = [
        pltpu.make_async_copy(r.okeep, r.okeep_o, r.store.at[7]),
        pltpu.make_async_copy(r.osend, r.osend_o, r.store.at[8]),
    ]
    for copy in more:
        copy.start()
    stores += more
    for j in range(1, slabs):
        moves[f"g{j}"].wait_recv()
    last = pltpu.make_async_copy(r.mgts, r.mgt_o, r.store.at[9])
    last.start()
    up_group.second()
    down_group.finish()
    up_group.finish()
    for copy in stores + [last]:
        copy.wait()
    total = slabs * heads
    for turn in (total - 2, total - 1):
        for copy in spills(turn // heads, turn % heads, turn % 2):
            copy.wait()
    for move in w.all:
        if move is not sent:
            move.wait_send()


def front(lens, x, og, vecs, f1b, f2b, vt, f1, f2, ow, up, down):
    rows, width = x.shape
    heads, _, longest = f2.shape
    depth = vt.shape[0]
    units = up.shape[1]
    slabs = lax.axis_size("head")
    osh = shard_shape(width, width)
    dsh = shard_shape(width, units)
    group = (slabs, rows, width)
    anywhere = pl.BlockSpec(memory_space=pl.ANY)
    vmem = pl.BlockSpec(memory_space=pltpu.VMEM)
    low = lambda *s: jax.ShapeDtypeStruct(s, BF16)
    wide = lambda *s: jax.ShapeDtypeStruct(s, F32)
    out_shape = [
        low(*group),
        low(slabs, width, rows),
        low(slabs, heads, rows, width),
        low(slabs, heads, rows, width),
        low(slabs, heads, rows, longest),
        low(slabs, depth, rows),
        low(slabs, depth, rows),
        low(*group),
        wide(rows, width),
        wide(rows, width),
        dsh,
        dsh,
        osh,
        osh,
        wide(1, units),
        wide(3, width),
    ]
    out_specs = [vmem if n in ("rg_o", "upb_sum", "sums") else anywhere for n in FRONT_OUT]
    vl = lambda *s: pltpu.VMEM(s, BF16)
    vw = lambda *s: pltpu.VMEM(s, F32)
    scratch = dict(
        xs=vl(*group),
        n1=vl(rows, width),
        n1t=vl(slabs, width, rows),
        f1v=vl(heads, width, width),
        f2v=vl(heads, width, longest),
        hidb=vl(2, rows, width),
        slopeb=vl(2, rows, width),
        probb=vl(2, rows, longest),
        valt=vl(slabs, depth, rows),
        mixt=vl(slabs, depth, rows),
        attt=vl(width, rows),
        owv=vl(width, width),
        upv=vl(width, units),
        downv=vl(units, width),
        ogs=vl(*group),
        n2s=vl(*group),
        act=vl(slabs, rows, units),
        pug=vl(slabs, rows, units),
        near1=vl(rows, width),
        near3=vl(rows, width),
        crossb=vl(rows, width),
        crossr=vl(rows, width),
        fterms=vl(*group),
        res=vw(rows, width),
        low=vl(rows, width),
        mgt=vl(width, rows),
        mgts=vl(slabs, depth, rows),
        acc=vw(width, width),
        dkeep=vl(*dsh.shape),
        dsend=vl(*dsh.shape),
        dgot=vl(*dsh.shape),
        ukeep=vl(*dsh.shape),
        usend=vl(*dsh.shape),
        ugot=vl(*dsh.shape),
        okeep=vl(*osh.shape),
        osend=vl(*osh.shape),
        send=pltpu.SemaphoreType.DMA((23 + 2 * osh.shape[0],)),
        recv=pltpu.SemaphoreType.DMA((23 + 2 * osh.shape[0],)),
        load=pltpu.SemaphoreType.DMA((5 + 2 * heads,)),
        spill=pltpu.SemaphoreType.DMA((2, 3)),
        store=pltpu.SemaphoreType.DMA((10,)),
    )
    smem = pl.BlockSpec(memory_space=pltpu.SMEM)
    return pl.pallas_call(
        front_kernel,
        out_shape=out_shape,
        in_specs=[smem] + [anywhere] * 2 + [vmem] * 4 + [anywhere] * 5,
        out_specs=out_specs,
        scratch_shapes=[scratch[n] for n in FRONT_SCRATCH],
        compiler_params=pltpu.CompilerParams(
            collective_id=0, has_side_effects=True, vmem_limit_bytes=FUSED_LIMIT
        ),
        cost_estimate=cost(
            slabs * rows * width * (heads * (width + longest) + 6 * units), 60 << 20
        ),
        name="front",
    )(lens, x, og, vecs, f1b, f2b, vt, f1, f2, ow, up, down)


BACK_IN = (
    "lens", "upb_sum", "sums", "hid", "slope", "prob", "n1t", "valt", "mgt", "f1", "f2", "vt",
    "xs", "fterms", "okeep", "osend",
)
BACK_OUT = (
    "t_o", "tnear_o", "tcross_o", "fnear_o", "fcross_o", "ow_o", "f1_o", "f2_o", "val_o",
    "small_o",
)
BACK_SCRATCH = (
    "n1tv", "valtv", "mgtv", "vgt", "f1v", "f2v", "vtv", "hidb", "slopeb", "probb", "sg", "pog",
    "acc1", "acc2", "acc3", "xb", "terms", "near3", "crossb", "fb", "fnear3", "ok", "ogot",
    "akeep", "asend", "agot", "bkeep", "bsend", "bgot", "vkeep", "vsend", "vgot", "small",
    "small_y", "small_z", "send", "recv", "load", "fetch", "store",
)


def back_kernel(*refs):
    r = types.SimpleNamespace(**dict(zip(BACK_IN + BACK_OUT + BACK_SCRATCH, refs)))
    slabs, heads, rows, width = r.pog.shape
    longest = r.probb.shape[2]
    depth = r.vgt.shape[1]
    dim = depth // heads
    blocks = rows // BLOCK
    count = r.ok.shape[0]
    me = lax.axis_index("head")
    turns = slabs * heads
    w = Wires(r.send, r.recv)
    out_group = Shards(w, r.ok, r.osend, r.ogot, r.ow_o, r.store.at[0])
    f1_group = [
        Shards(w, r.akeep.at[h], r.asend.at[h], r.agot.at[h], r.f1_o.at[h], r.store.at[1 + h])
        for h in range(heads)
    ]
    f2_group = [
        Shards(
            w, r.bkeep.at[h], r.bsend.at[h], r.bgot.at[h], r.f2_o.at[h], r.store.at[1 + heads + h]
        )
        for h in range(heads)
    ]
    val_group = Shards(w, r.vkeep, r.vsend, r.vgot, r.val_o, r.store.at[1 + 2 * heads])
    fterm1 = w.remote(r.fterms.at[1], r.fnear_o, "head", 1)
    fterm3 = w.remote(r.fterms.at[3], r.fnear3, "head", 1)
    fcross = w.remote(r.fb, r.fcross_o, "head", 2)
    term1 = w.remote(r.terms.at[1], r.tnear_o, "head", 1)
    term3 = w.remote(r.terms.at[3], r.near3, "head", 1)
    cross = w.remote(r.crossb, r.tcross_o, "head", 2)
    small_y = w.remote(r.small, r.small_y, "dp", 1)
    small_z = [
        w.remote(r.small_z.at[0], r.small_z.at[k], "dp", 2 * k) for k in range(1, count)
    ]
    small_x = [
        w.remote(r.small, r.small_o.at[j], "head", j) for j in range(1, slabs)
    ]
    own_term = pltpu.make_async_copy(r.terms.at[0], r.t_o, r.store.at[2 + 2 * heads])
    own_small = pltpu.make_async_copy(r.small, r.small_o.at[0], r.store.at[3 + 2 * heads])

    def load(index, src, dst):
        return pltpu.make_async_copy(src, dst, r.load.at[index])

    loads = [
        load(0, r.mgt, r.mgtv),
        load(1, r.valt, r.valtv),
        load(2, r.f2, r.f2v),
        load(3, r.n1t, r.n1tv),
        load(4, r.okeep, r.ok),
        load(5, r.fterms.at[2], r.fb),
        load(6, r.f1, r.f1v),
        load(7, r.vt, r.vtv),
        load(8, r.xs.at[3], r.xb),
    ]

    def fetches(turn):
        h, j, slot = turn // slabs, turn % slabs, turn % 2
        return [
            pltpu.make_async_copy(r.prob.at[j, h], r.probb.at[slot], r.fetch.at[slot, 0]),
            pltpu.make_async_copy(r.slope.at[j, h], r.slopeb.at[slot], r.fetch.at[slot, 1]),
            pltpu.make_async_copy(r.hid.at[j, h], r.hidb.at[slot], r.fetch.at[slot, 2]),
        ]

    for copy in loads[:2] + fetches(0) + loads[2:]:
        copy.start()
    greet(partners())
    out_group.start()
    fterm3.start()
    fterm1.start()
    r.small[...] = jnp.zeros_like(r.small)
    r.small[2 * heads : 2 * heads + 1] = r.upb_sum[...]
    r.small[2 * heads + 3 : 2 * heads + 6] = r.sums[...]
    for copy in loads[:6]:
        copy.wait()

    def turn_step(turn, carry):
        h, j, slot = turn // slabs, turn % slabs, turn % 2
        for copy in fetches(turn):
            copy.wait()

        @pl.when(turn + 1 < turns)
        def _():
            for copy in fetches(turn + 1):
                copy.start()

        @pl.when(j == 0)
        def _():
            r.acc1[...] = jnp.zeros_like(r.acc1)
            r.acc2[...] = jnp.zeros_like(r.acc2)

        head_rows = pl.ds(pl.multiple_of(h * dim, dim), dim)
        mgt = r.mgtv[j, head_rows]
        r.vgt[j, head_rows] = mm(mgt, r.probb[slot]).astype(BF16)
        probs_grad = mm_tn(mgt, r.valtv[j, head_rows])
        first = jnp.bitwise_xor(me, j) * blocks
        zero = jnp.zeros((BLOCK, BLOCK), F32)
        for b in range(blocks):
            length = r.lens[first + b]
            own = slice(b * BLOCK, (b + 1) * BLOCK)
            prob = r.probb[slot, own].astype(F32)
            grad = probs_grad[own]
            inner = jnp.sum(prob * grad, -1, keepdims=True)
            parts = cells(prob * (grad - inner))
            is_full = length == longest
            is_half = length == longest // 2
            for c in range(blocks):
                half = parts[2 * (b // 2) + c] if c < 2 else zero
                quarter = parts[b] if c == 0 else zero
                cell = jnp.where(is_full, parts[c], jnp.where(is_half, half, quarter))
                r.sg[own, c * BLOCK : (c + 1) * BLOCK] = cell.astype(BF16)
        scores_grad = r.sg[...]
        row = pl.ds(h, 1)
        pog = (mm_nt(scores_grad, r.f2v[h]) * r.slopeb[slot].astype(F32)).astype(BF16)
        r.pog[j, h] = pog
        r.small[row] += jnp.sum(pog.astype(F32), 0, keepdims=True)
        row = pl.ds(heads + h, 1)
        r.small[row, 0:longest] += jnp.sum(scores_grad.astype(F32), 0, keepdims=True)
        r.acc2[...] += mm_tn(r.hidb[slot], scores_grad)
        r.acc1[...] += mm(r.n1tv[j], pog)

        for k in range(heads):

            @pl.when(turn == slabs * k + slabs - 1)
            def _(k=k):
                store_shards(r.bkeep.at[k], r.bsend.at[k], slice(None), r.acc2)
                if k < heads - 1:
                    f2_group[k].start()
                store_shards(r.akeep.at[k], r.asend.at[k], slice(None), r.acc1)
                if k < heads - 1:
                    f1_group[k].start()

        @pl.when(turn == 1)
        def _():
            fterm3.wait_recv()
            r.fb[...] = add_low(r.fb[...], r.fnear3[...])
            fcross.start()

        @pl.when(turn == slabs + 1)
        def _():
            out_group.second()

        return carry

    lax.fori_loop(0, turns, turn_step, 0)
    f2_group[0].second()
    f1_group[0].second()
    for copy in loads[6:]:
        copy.wait()

    def term_step(i, carry):
        j = slabs - 1 - i

        @pl.when(i > 0)
        def _():
            load(8, r.xs.at[j], r.xb).wait()

        term = mm_tn(r.vgt[j], r.vtv[...])
        for h in range(heads):
            term += mm_nt(r.pog[j, h], r.f1v[h])
        low = term.astype(BF16)
        r.terms[j] = low
        wide = low.astype(F32)
        scaled, _ = standardize(r.xb[...].astype(F32))
        base = 2 * heads + 1
        r.small[base : base + 1] += jnp.sum(wide * scaled, 0, keepdims=True)
        r.small[base + 1 : base + 2] += jnp.sum(wide, 0, keepdims=True)

        @pl.when(i < slabs - 1)
        def _():
            load(8, r.xs.at[j - 1], r.xb).start()

        @pl.when(i == 0)
        def _():
            term3.start()

        @pl.when(i == 1)
        def _():
            term3.wait_recv()
            r.crossb[...] = add_low(r.terms[2], r.near3[...])
            cross.start()

        @pl.when(i == 2)
        def _():
            term1.start()

        return carry

    lax.fori_loop(0, slabs, term_step, 0)
    own_term.start()
    small_y.start()
    f2_group[-1].start()
    f1_group[-1].start()
    flat = (depth, slabs * rows)
    total = mm_nt(r.n1tv[0], r.vgt[0])
    for j in range(1, slabs):
        total += mm_nt(r.n1tv[j], r.vgt[j])
    r.acc3[...] = total
    store_shards(r.vkeep, r.vsend, slice(None), r.acc3)
    val_group.start()
    for h in range(1, heads - 1):
        f2_group[h].second()
        f1_group[h].second()
    small_y.wait_recv()
    r.small_z[0] = r.small[...] + r.small_y[...]
    for move in small_z:
        move.start()
    f2_group[-1].second()
    for move in small_z:
        move.wait_recv()
    small_y.wait_send()
    r.small[...] = sum(r.small_z[k] for k in range(count))
    for move in small_x:
        move.start()
    own_small.start()
    f1_group[-1].second()
    val_group.second()
    for group in [out_group] + f1_group + f2_group + [val_group]:
        group.finish()
    for move in [fterm1, fcross, term1, cross] + small_x:
        move.wait_recv()
    own_term.wait()
    own_small.wait()
    for move in w.all:
        if move is not small_y:
            move.wait_send()


def low_shape(*shape):
    return jax.ShapeDtypeStruct(shape, BF16)


def wide_shape(*shape):
    return jax.ShapeDtypeStruct(shape, F32)


def back(lens, upb_sum, sums, hid, slope, prob, n1t, valt, mgt, f1, f2, vt, xs, fterms, okeep, osend):
    slabs, heads, rows, width = hid.shape
    longest = f2.shape[2]
    depth = vt.shape[0]
    count, part, _ = okeep.shape
    small = (2 * heads + 6 + 7) // 8 * 8
    low, wide = low_shape, wide_shape
    out_shape = [
        low(rows, width),
        low(rows, width),
        low(rows, width),
        low(rows, width),
        low(rows, width),
        low(count, part, width),
        low(heads, count, part, width),
        low(heads, count, part, longest),
        low(count, part, depth),
        wide(slabs, small, width),
    ]
    vl = lambda *s: pltpu.VMEM(s, BF16)
    vw = lambda *s: pltpu.VMEM(s, F32)
    moves = 4 + (count - 1) + (2 * heads + 2) * count + 6
    scratch = dict(
        n1tv=vl(slabs, width, rows),
        valtv=vl(slabs, depth, rows),
        mgtv=vl(slabs, depth, rows),
        vgt=vl(slabs, depth, rows),
        f1v=vl(heads, width, width),
        f2v=vl(heads, width, longest),
        vtv=vl(depth, width),
        hidb=vl(2, rows, width),
        slopeb=vl(2, rows, width),
        probb=vl(2, rows, longest),
        sg=vl(rows, longest),
        pog=vl(slabs, heads, rows, width),
        acc1=vw(width, width),
        acc2=vw(width, longest),
        acc3=vw(width, depth),
        xb=vl(rows, width),
        terms=vl(slabs, rows, width),
        near3=vl(rows, width),
        crossb=vl(rows, width),
        fb=vl(rows, width),
        fnear3=vl(rows, width),
        ok=vl(count, part, width),
        ogot=vl(count, part, width),
        akeep=vl(heads, count, part, width),
        asend=vl(heads, count, part, width),
        agot=vl(heads, count, part, width),
        bkeep=vl(heads, count, part, longest),
        bsend=vl(heads, count, part, longest),
        bgot=vl(heads, count, part, longest),
        vkeep=vl(count, part, depth),
        vsend=vl(count, part, depth),
        vgot=vl(count, part, depth),
        small=vw(small, width),
        small_y=vw(small, width),
        small_z=vw(count, small, width),
        send=pltpu.SemaphoreType.DMA((moves,)),
        recv=pltpu.SemaphoreType.DMA((moves,)),
        load=pltpu.SemaphoreType.DMA((9,)),
        fetch=pltpu.SemaphoreType.DMA((2, 3)),
        store=pltpu.SemaphoreType.DMA((4 + 2 * heads,)),
    )
    smem = pl.BlockSpec(memory_space=pltpu.SMEM)
    anywhere = pl.BlockSpec(memory_space=pl.ANY)
    vmem = pl.BlockSpec(memory_space=pltpu.VMEM)
    return pl.pallas_call(
        back_kernel,
        out_shape=out_shape,
        in_specs=[smem, vmem, vmem] + [anywhere] * 13,
        out_specs=[anywhere] * len(out_shape),
        scratch_shapes=[scratch[n] for n in BACK_SCRATCH],
        compiler_params=pltpu.CompilerParams(
            collective_id=1, has_side_effects=True, vmem_limit_bytes=FUSED_LIMIT
        ),
        cost_estimate=cost(slabs * rows * width * heads * (3 * width + 2 * longest), 60 << 20),
        name="back",
    )(lens, upb_sum, sums, hid, slope, prob, n1t, valt, mgt, f1, f2, vt, xs, fterms, okeep, osend)


def finish_kernel(*refs):
    (
        t0, t1, t2, x, rg, gain, e0, e1, e2, res, downb, small, down, up, ow, f1, f2, val,
    ) = refs[:18]
    (
        result_o, input_o, f1b_o, f2b_o, upb_o, shared_o, down_o, up_o, ow_o, f1_o, f2_o, val_o,
    ) = refs[18:]
    add3 = lambda a, b, c: a[...].astype(F32) + b[...].astype(F32) + c[...].astype(F32)
    result_o[...] = res[...] + (add3(e0, e1, e2) + downb[...])
    scaled, inv_std = standardize(x[...].astype(F32))
    input_o[...] = rg[...] + norm_back(add3(t0, t1, t2), scaled, inv_std, gain[...])
    slabs = small.shape[0]
    heads = f1.shape[0]
    longest = f2.shape[3]
    count = f1.shape[1]
    me = lax.axis_index("head")
    for j in range(slabs):
        owner = jnp.bitwise_xor(me, j)
        upb_o[pl.ds(owner, 1)] = small[j, 2 * heads : 2 * heads + 1]
        for h in range(heads):
            f1b_o[pl.ds(owner * heads + h, 1)] = small[j, h : h + 1]
            f2b_o[pl.ds(owner * heads + h, 1)] = small[j, heads + h : heads + h + 1, 0:longest]
    first = 2 * heads + 1
    shared_o[...] = sum(small[j, first : first + 5] for j in range(slabs))
    for src, dst in ((down, down_o), (up, up_o), (ow, ow_o), (val, val_o)):
        dst[...] = sum(src[k].astype(F32) for k in range(count))
    for h in range(heads):
        f1_o[h] = sum(f1[h, k].astype(F32) for k in range(count))
        f2_o[h] = sum(f2[h, k].astype(F32) for k in range(count))


def finish(members, *args):
    t0, f1, f2, val = args[0], args[15], args[16], args[17]
    rows, width = t0.shape
    heads, _, part, longest = f2.shape
    wide = wide_shape
    return pl.pallas_call(
        finish_kernel,
        out_shape=[
            wide(rows, width),
            wide(rows, width),
            wide(members * heads, width),
            wide(members * heads, longest),
            wide(members, width),
            wide(5, width),
            wide(part, width),
            wide(part, width),
            wide(part, width),
            wide(heads, part, width),
            wide(heads, part, longest),
            wide(part, val.shape[2]),
        ],
        compiler_params=pltpu.CompilerParams(vmem_limit_bytes=VMEM_LIMIT),
        cost_estimate=cost(0, 20 << 20),
        name="finish",
    )(*args)


def local(
    tokens,
    seq_len,
    norm1_gain,
    norm1_bias,
    f1_weight,
    f1_bias,
    f2_weight,
    f2_bias,
    value_weight,
    out_weight,
    norm2_gain,
    norm2_bias,
    up_weight,
    up_bias,
    down_weight,
    down_bias,
    out_grad,
):
    members = lax.axis_size("head")
    vt = value_weight.T
    vecs = jnp.stack([norm1_gain, norm1_bias, norm2_gain, norm2_bias, up_bias, down_bias])
    (
        xs, n1t, hid, slope, prob, valt, mgt, fterms, res_grad, residual, down_parts, up_parts,
        out_keep, out_send, upb, sums2,
    ) = front(
        seq_len, tokens, out_grad, vecs, f1_bias, f2_bias, vt, f1_weight, f2_weight, out_weight,
        up_weight, down_weight,
    )
    (
        t0, tnear, tcross, fnear, fcross, ow_parts, f1_parts, f2_parts, val_parts, small,
    ) = back(
        seq_len, upb, sums2, hid, slope, prob, n1t, valt, mgt, f1_weight, f2_weight, vt, xs,
        fterms, out_keep, out_send,
    )
    (
        result, input_grad, f1b_all, f2b_all, upb_all, shared, down_t, up_piece, ow_piece,
        f1_piece, f2_piece, value_piece,
    ) = finish(
        members, t0, tnear, tcross, tokens, res_grad, vecs[0:1], fterms[0], fnear, fcross,
        residual, vecs[5:6], small, down_parts, up_parts, ow_parts, f1_parts, f2_parts, val_parts,
    )
    low = ow_piece.astype(BF16)
    low = add_low(low, swap(low, "head", 1))
    out_piece = low.astype(F32) + swap(low, "head", 2).astype(F32)
    return (
        result,
        input_grad,
        shared[0],
        shared[1],
        f1_piece,
        f1b_all,
        f2_piece,
        f2b_all,
        value_piece,
        out_piece,
        shared[2],
        shared[3],
        up_piece,
        upb_all.reshape(-1),
        down_t.T,
        shared[4],
    )


def solution(mesh):
    placed = (
        P(("dp", "head"), None),
        P("dp"),
        P(),
        P(),
        P("head", None, None),
        P("head", None),
        P("head", None, None),
        P("head", None),
        P(None, "head"),
        P(),
        P(),
        P(),
        P(None, "head"),
        P("head"),
        P("head", None),
        P(),
        P(("dp", "head"), None),
    )
    return jax.shard_map(
        local,
        mesh=mesh,
        in_specs=placed,
        out_specs=(
            P(("dp", "head"), None),
            P(("dp", "head"), None),
            P(),
            P(),
            P("head", "dp", None),
            P(),
            P("head", "dp", None),
            P(),
            P("dp", "head"),
            P("dp", None),
            P(),
            P(),
            P("dp", "head"),
            P(),
            P("head", "dp"),
            P(),
        ),
        check_vma=False,
    )
```

profile of v0, /device:TPU:0, one launch (start us, length us, event | category | flops | bytes accessed | tf_op | source)
XLA Modules:
  0.0 258.0 jit_solution(17413860154713862537)
XLA Ops:
  0.6 0.7 stack.21.refs_5_
  1.3 0.7 stack.26.refs_10_
  2.0 0.7 stack.22
  2.7 0.7 stack.23
  3.4 0.7 stack.24
  4.1 0.7 stack.25
  4.8 0.6 stack.27.refs_3_
  5.4 120.4 %front.1 = (bf16[4,512,768]{2,1,0:T(8,128)(2,1)}, bf16[4,768,512]{2,1,0:T(8,128)(2,1)}, bf16[4,3,512,768]{3,2,1,0:T(8,128)(2,1)}, bf16[4,3,512,768]{3,2,1,0:T(8,...) custom-call(s32[16]{0:T(128)} %refs_0_.3, ...), custom_call_target="tpu_custom_call" | custom-call | flops 26575110144 | bytes 62914560 | tf_op jit(solution)/shard_map/front/pallas_call | solution.py:545
  125.8 2.1 slice_bitcast_fusion.refs_6_
  127.9 0.0 copy-start.2
  127.9 0.0 copy-start.3
  127.9 108.9 %back.1 = (bf16[512,768]{1,0:T(8,128)(2,1)}, bf16[512,768]{1,0:T(8,128)(2,1)}, bf16[512,768]{1,0:T(8,128)(2,1)}, bf16[512,768]{1,0:T(8,128)(2,1)}, bf16[512,768]...) custom-call(s32[16]{0:T(128)} %refs_0_.3, ...), custom_call_target="tpu_custom_call" | custom-call | flops 31406948352 | bytes 62914560 | tf_op jit(solution)/shard_map/back/pallas_call | solution.py:878
  236.8 0.0 copy-done.2
  236.8 0.0 copy-done.3
  236.8 0.0 copy-start
  236.8 1.1 copy-done
  238.0 0.0 copy-start.1
  238.0 1.1 copy-done.1
  239.1 0.0 copy-start.4
  239.1 1.1 copy-done.4
  240.2 0.0 copy-start.5
  240.2 0.9 copy-done.5
  241.1 0.0 copy-start.6
  241.1 0.9 copy-done.6
  242.0 7.8 %finish.1 = (f32[512,768]{1,0:T(8,128)}, f32[512,768]{1,0:T(8,128)}, f32[12,768]{1,0:T(8,128)}, f32[12,512]{1,0:T(8,128)}, f32[4,768]{1,0:T(4,128)S(1)}, /*index...) custom-call(bf16[512,768]{1,0:T(8,128)(2,1)S(1)} %copy-done, ...), custom_call_target="tpu_custom_call" | custom-call | bytes 20971520 | tf_op jit(solution)/shard_map/finish/pallas_call | solution.py:928
  249.8 0.1 collective-permute-start
  249.9 1.4 collective-permute-done
  251.3 0.6 collective-permute-start.1
  251.9 0.6 reshape.35
  252.5 0.6 slice_reduce_fusion
  253.1 4.1 %collective-permute-done.1 = bf16[96,768]{1,0:T(8,128)(2,1)S(1)} collective-permute-done((bf16[96,768]{1,0:T(8,128)(2,1)S(1)}, bf16[96,768]{1,0:T(8,128)(2,1)S(1)}, u32[]{:S(2)}, u32[]{:S(2)}) %collective-permute-start.1) | collective-permute-done | bytes 147488 | tf_op jit(solution)/shard_map/ppermute | solution.py:53
  257.2 0.7 convert_add_fusion
  (2 shorter events, 0.0 us)
Async XLA Ops:
  127.9 108.9 %copy-start.2 = (bf16[4,96,768]{2,1,0:T(8,128)(2,1)S(1)}, bf16[4,96,768]{2,1,0:T(8,128)(2,1)}, u32[]{:S(2)}) copy-start(bf16[4,96,768]{2,1,0:T(8,128)(2,1)} %get-tuple-element.74.refs_12_) | copy-start | bytes 1769476
  127.9 108.9 %copy-start.3 = (bf16[4,96,768]{2,1,0:T(8,128)(2,1)S(1)}, bf16[4,96,768]{2,1,0:T(8,128)(2,1)}, u32[]{:S(2)}) copy-start(bf16[4,96,768]{2,1,0:T(8,128)(2,1)} %get-tuple-element.75.refs_13_) | copy-start | bytes 1769476
  236.8 1.1 copy-start
  238.0 1.1 copy-start.1
  239.1 1.1 copy-start.4
  240.2 0.9 copy-start.5
  241.1 0.9 copy-start.6
  249.8 1.4 collective-permute-start
  251.3 6.0 %collective-permute-start.1 = (bf16[96,768]{1,0:T(8,128)(2,1)S(1)}, bf16[96,768]{1,0:T(8,128)(2,1)S(1)}, u32[]{:S(2)}, u32[]{:S(2)}) collective-permute-start(bf16[96,768]{1,0:T(8,128)(2,1)S(1)} %add_convert_fusion), channel_id=1, source_target_pairs={{0,2},{1,3},{2,0},{3,1},{4,6},{5,7},{6,4},{7,5},{8,10},{9,11},{10,... | collective-permute-start | bytes 442376 | tf_op jit(solution)/shard_map/ppermute | solution.py:53
where the time goes:
time: 259 us; the launch traced here: 258 us
  Pallas kernels  237 us (92%)
  local copies, waits for them, and re-layouts  13.3 us (5%)
  waiting for transfers between devices  5.47 us (2%)
    pallas_call x1, Pallas kernels, front(): pl.pallas_call(front_kernel, out_shape=out_shape, in_specs=[smem] + [anyw...  120 us
    pallas_call x1, Pallas kernels, back(): pl.pallas_call(back_kernel, out_shape=out_shape, in_specs=[smem, vmem, vm...  109 us
    pallas_call x1, Pallas kernels, finish(): pl.pallas_call(finish_kernel, out_shape=[wide(rows, width), wide(rows, wi...  7.77 us
    ppermute x2, waiting for transfers between devices, swap(): lax.ppermute(value, axis, [(i, i ^ step) for i in range(lax.axis_size(axi...  5.47 us
    unnamed x14, local copies, waits for them, and re-layouts  5.18 us
  transfers between devices with their start and end apart: 2, of which 2 were waited for; matrix products, arithmetic and copies ran while one was open for 0% of the time, Pallas kernels for 0%

commit v1 on v0

v1 whole, which is shorter than its diff:
```python
import types

import jax
import jax.numpy as jnp
from jax import lax
from jax.experimental import pallas as pl
from jax.experimental.pallas import tpu as pltpu
from jax.sharding import PartitionSpec as P

F32 = jnp.float32
BF16 = jnp.bfloat16
BLOCK = 128
FUSED_LIMIT = 63 << 20


def mm(a, b):
    return lax.dot_general(a, b, (((1,), (0,)), ((), ())), preferred_element_type=F32)


def mm_nt(a, b):
    return lax.dot_general(a, b, (((1,), (1,)), ((), ())), preferred_element_type=F32)


def mm_tn(a, b):
    return lax.dot_general(a, b, (((0,), (0,)), ((), ())), preferred_element_type=F32)


def standardize(values):
    centred = values - jnp.mean(values, -1, keepdims=True)
    inv_std = lax.rsqrt(jnp.mean(centred * centred, -1, keepdims=True) + 1e-05)
    return centred * inv_std, inv_std


def norm_back(grad_out, scaled, inv_std, gain):
    grad_scaled = grad_out * gain
    centre_mean = jnp.mean(grad_scaled, -1, keepdims=True)
    cross_mean = jnp.mean(grad_scaled * scaled, -1, keepdims=True)
    return inv_std * (grad_scaled - centre_mean - scaled * cross_mean)


def silu_and_slope(pre_val):
    sigma = 0.5 + 0.5 * jnp.tanh(0.5 * pre_val)
    gated = pre_val * sigma
    return gated, sigma + gated * (1.0 - sigma)


def add_low(a, b):
    return (a.astype(F32) + b.astype(F32)).astype(BF16)


def cost(macs, bytes_accessed):
    return pl.CostEstimate(flops=2 * macs, bytes_accessed=bytes_accessed, transcendentals=0)


def store_shards(both, acc):
    _, count, depth, _ = both.shape
    me = lax.axis_index("dp")
    for d in range(2 * count):
        side = jnp.bitwise_xor(me % 2, d % 2)
        place = jnp.bitwise_xor(me // 2, d // 2)
        both[side, place] = acc[d * depth : (d + 1) * depth].astype(BF16)


def shard_shape(width, lanes):
    members = lax.axis_size("dp")
    return jax.ShapeDtypeStruct((2, members // 2, width // members, lanes), BF16)


class Wires:
    def __init__(self, send, recv):
        self.send, self.recv, self.used = send, recv, 0
        self.all = []

    def remote(self, src, dst, axis, step):
        index = self.used
        self.used += 1
        move = pltpu.make_async_remote_copy(
            src_ref=src,
            dst_ref=dst,
            send_sem=self.send.at[index],
            recv_sem=self.recv.at[index],
            device_id={axis: jnp.bitwise_xor(lax.axis_index(axis), step)},
            device_id_type=pl.DeviceIdType.MESH,
        )
        self.all.append(move)
        return move


class Shards:
    def __init__(self, wires, keep, send, got, out, local_sem):
        self.keep, self.got = keep, got
        self.count = keep.shape[0]
        self.first = wires.remote(send, got, "dp", 1)
        self.rest = [
            wires.remote(keep.at[k], out.at[k], "dp", 2 * k) for k in range(1, self.count)
        ]
        self.own = pltpu.make_async_copy(keep.at[0], out.at[0], local_sem)

    def start(self):
        self.first.start()

    def second(self):
        self.first.wait_recv()
        for k in list(range(1, self.count)) + [0]:
            self.keep[k] = add_low(self.keep[k], self.got[k])
            (self.rest[k - 1] if k else self.own).start()

    def finish(self):
        for move in self.rest:
            move.wait_recv()
        self.own.wait()


def add_got(keep, got):
    for k in range(keep.shape[0]):
        keep[k] = add_low(keep[k], got[k])


def greet(axes):
    barrier = pltpu.get_barrier_semaphore()
    for axis, step in axes:
        pl.semaphore_signal(
            barrier,
            1,
            device_id={axis: jnp.bitwise_xor(lax.axis_index(axis), step)},
            device_id_type=pl.DeviceIdType.MESH,
        )
    pl.semaphore_wait(barrier, len(axes))


def partners():
    over_dp = [1] + list(range(2, lax.axis_size("dp"), 2))
    return [("head", s) for s in range(1, lax.axis_size("head"))] + [("dp", s) for s in over_dp]


FRONT_IN = (
    "lens", "x", "og", "gain1", "bias1", "gain2", "bias2", "upb", "f1b", "f2b", "vw", "f1", "f2",
    "ow", "up", "down",
)
FRONT_OUT = (
    "xs_o", "n1t_o", "hid_o", "slope_o", "prob_o", "valt_o", "mgt_o", "f_o", "rg_o", "res_o",
    "down_o", "up_o", "ow_o", "upb_sum", "sums",
)
FRONT_SCRATCH = (
    "xs", "n1", "n1t", "big", "f2v", "vwv", "hidb", "slopeb", "probb", "valt", "attt", "owv", "upv",
    "downv", "ogs", "n2s", "pug", "near1", "near3", "crossb", "crossr", "fterms", "res", "mgts",
    "acc", "vt", "ohalf", "osent", "ogot", "dboth", "dgot", "uboth", "oboth", "send", "recv",
    "load", "spill", "store",
)


def flat_row(ref):
    return ref[...].reshape(1, -1)


def split_prob(parts, length, longest, b, zero):
    is_full = length == longest
    is_half = length == longest // 2
    for c in range(len(parts)):
        half = parts[c % 2] if c // 2 == b // 2 else zero
        quarter = parts[0] if c == b else zero
        yield c, jnp.where(is_full, parts[c], jnp.where(is_half, half, quarter))


def cells(row):
    return [row[:, c : c + BLOCK] for c in range(0, row.shape[1], BLOCK)]


def front_kernel(*refs):
    r = types.SimpleNamespace(**dict(zip(FRONT_IN + FRONT_OUT + FRONT_SCRATCH, refs)))
    r.low = r.n1
    r.terms = r.xs
    slabs, rows, width = r.xs.shape
    heads, _, longest = r.f2v.shape
    depth = r.valt.shape[1]
    dim = depth // heads
    half = rows // 2
    blocks = rows // BLOCK
    me = lax.axis_index("head")

    w = Wires(r.send, r.recv)
    down_first = w.remote(r.dboth.at[1], r.dgot, "dp", 1)

    def remote(src, dst, step):
        return w.remote(src, dst, "head", step)

    def cut(c):
        return pl.ds(c * half, half)

    def share(step):
        return pl.ds(pl.multiple_of(jnp.bitwise_xor(me, step) * depth, depth), depth)

    my_rows = share(0)
    r.mgt = r.n1t.at[0]
    moves = {
        "x1": remote(r.x, r.xs.at[1], 1),
        "x2": remote(r.x, r.xs.at[2], 2),
        "x3": remote(r.xs.at[2], r.xs.at[3], 1),
        "o1": remote(r.og, r.ogs.at[1], 1),
        "o2": remote(r.og, r.ogs.at[2], 2),
        "o3": remote(r.ogs.at[2], r.ogs.at[3], 1),
        "t1": remote(r.terms.at[1], r.near1, 1),
    }
    columns = remote(r.osent, r.ogot, 1)
    near, far, onward = [], [], []
    for j in range(slabs):
        near.append(remote(r.attt.at[j, my_rows], r.attt.at[j ^ 1, my_rows], 1))
        far.append(remote(r.attt.at[j, my_rows], r.attt.at[j ^ 2, my_rows], 2))
        onward.append(remote(r.attt.at[j, share(2)], r.attt.at[j ^ 1, share(2)], 1))
    for j in range(1, slabs):
        moves[f"g{j}"] = remote(r.mgt.at[share(j)], r.mgts.at[j], j)
    for c in range(2):
        part = cut(c)
        moves[f"t3{c}"] = remote(r.terms.at[3, part], r.near3.at[part], 1)
        moves[f"c{c}"] = remote(r.crossb.at[part], r.crossr.at[part], 2)

    def f1_load(h):
        rows_of = pl.ds(pl.multiple_of(h * width, width), width)
        return pltpu.make_async_copy(r.f1.at[h], r.big.at[rows_of], r.load.at[1 + 2 * h])

    def f2_load(h):
        return pltpu.make_async_copy(r.f2.at[h], r.f2v.at[h], r.load.at[2 + 2 * h])

    loads = [pltpu.make_async_copy(r.x, r.xs.at[0], r.load.at[0])]
    for h in range(heads):
        loads += [f1_load(h), f2_load(h)]
    base = 1 + 2 * heads
    late = [
        pltpu.make_async_copy(r.ow, r.owv, r.load.at[base]),
        pltpu.make_async_copy(r.up, r.upv, r.load.at[base + 1]),
        pltpu.make_async_copy(r.down, r.downv, r.load.at[base + 2]),
        pltpu.make_async_copy(r.og, r.ogs.at[0], r.load.at[base + 3]),
    ]
    columns_load = pltpu.make_async_copy(r.vw, r.vwv, r.load.at[base + 4])
    columns_load.start()
    for copy in loads:
        copy.start()
    greet(partners())
    moves["x2"].start()
    moves["x1"].start()
    for copy in late:
        copy.start()
    columns_load.wait()
    r.vt[...] = r.vwv[...].T
    loads[0].wait()

    def spills(j, h, slot):
        return [
            pltpu.make_async_copy(r.hidb.at[slot], r.hid_o.at[j, h], r.spill.at[slot, 0]),
            pltpu.make_async_copy(r.slopeb.at[slot], r.slope_o.at[j, h], r.spill.at[slot, 1]),
            pltpu.make_async_copy(r.probb.at[slot], r.prob_o.at[j, h], r.spill.at[slot, 2]),
        ]

    def slab_step(j, carry):
        @pl.when(j == 1)
        def _():
            moves["x1"].wait_recv()

        @pl.when(j == 2)
        def _():
            moves["x2"].wait_recv()
            moves["x3"].start()
            moves["o2"].start()
            moves["o1"].start()

        @pl.when(j == 3)
        def _():
            moves["x3"].wait_recv()
            for k in range(2):
                far[k].wait_recv()
                onward[k ^ 2].start()

        scaled, _ = standardize(r.xs[j].astype(F32))
        low = (scaled * flat_row(r.gain1) + flat_row(r.bias1)).astype(BF16)
        r.n1[...] = low
        r.n1t[j] = low.T
        r.valt[j] = mm(r.vt[...], r.n1t[j]).astype(BF16)

        def head_step(h, carry):
            turn = j * heads + h
            slot = turn % 2

            @pl.when(j == 0)
            def _():
                f1_load(h).wait()
                f2_load(h).wait()

            @pl.when(turn >= 2)
            def _():
                for copy in spills(j, h, slot):
                    copy.wait()

            first = jnp.bitwise_xor(me, j) * blocks
            column = lax.broadcasted_iota(jnp.int32, (BLOCK, longest), 1)
            zero = jnp.zeros((BLOCK, BLOCK), F32)
            f1_rows = pl.ds(pl.multiple_of(h * width, width), width)
            for c in range(2):
                part = slice(c * half, (c + 1) * half)
                gated, slope = silu_and_slope(mm(r.n1[part], r.big[f1_rows]) + r.f1b[pl.ds(h, 1)])
                hidden = gated.astype(BF16)
                r.hidb[slot, part] = hidden
                r.slopeb[slot, part] = slope.astype(BF16)
                scores = mm(hidden, r.f2v[h]) + r.f2b[pl.ds(h, 1)]
                for i in range(half // BLOCK):
                    b = c * (half // BLOCK) + i
                    length = r.lens[first + b]
                    own = scores[i * BLOCK : (i + 1) * BLOCK]
                    keep = column < length
                    top = jnp.max(jnp.where(keep, own, -3.0e38), -1, keepdims=True)
                    exp_val = jnp.where(keep, jnp.exp(own - top), 0.0)
                    prob = exp_val * (1.0 / jnp.sum(exp_val, -1, keepdims=True))
                    for k, cell in split_prob(cells(prob), length, longest, b, zero):
                        r.probb[
                            slot, b * BLOCK : (b + 1) * BLOCK, k * BLOCK : (k + 1) * BLOCK
                        ] = cell.astype(BF16)
            own_rows = pl.ds(pl.multiple_of(h * dim, dim), dim)
            mixed = mm_nt(r.valt[j, own_rows], r.probb[slot])
            place = pl.ds(pl.multiple_of(me * depth + h * dim, dim), dim)
            r.attt[j, place] = mixed.astype(BF16)
            for copy in spills(j, h, slot):
                copy.start()
            return carry

        lax.fori_loop(0, heads, head_step, 0)
        for k in range(slabs):

            @pl.when(j == k)
            def _(k=k):
                far[k].start()
                near[k].start()

        return carry

    lax.fori_loop(0, slabs, slab_step, 0)
    stores = [
        pltpu.make_async_copy(r.xs, r.xs_o, r.store.at[0]),
        pltpu.make_async_copy(r.n1t, r.n1t_o, r.store.at[1]),
        pltpu.make_async_copy(r.valt, r.valt_o, r.store.at[2]),
    ]
    for copy in stores:
        copy.start()
    for k in (2, 3):
        near[k].wait_recv()
        onward[k].wait_recv()
    for copy in late:
        copy.wait()
    for copy in stores:
        copy.wait()
    stores = []
    sent = moves["x3"]
    sent.wait_send()

    def residual_step(j, carry):
        residual = r.xs[j].astype(F32) + mm_tn(r.attt[j], r.owv[...])

        @pl.when(j == 0)
        def _():
            r.res[...] = residual

        scaled, _ = standardize(residual)
        r.n2s[j] = (scaled * flat_row(r.gain2) + flat_row(r.bias2)).astype(BF16)
        return carry

    lax.fori_loop(2, 4, residual_step, 0)
    moves["o2"].wait_recv()
    moves["o3"].start()

    def ffn_step(u, carry):
        j = jnp.where(u < 4, 2 + u % 2, (u - 4) // 2)
        c = jnp.where(u < 4, u // 2, u % 2)

        @pl.when(u == 1)
        def _():
            moves["o3"].wait_recv()

        @pl.when(u == 2)
        def _():
            for k in (2, 3):
                far[k].wait_recv()
                onward[k ^ 2].start()

        @pl.when(u == 4)
        def _():
            for k in (0, 1):
                near[k].wait_recv()
                onward[k].wait_recv()
            moves["o1"].wait_recv()
            lax.fori_loop(0, 2, residual_step, 0)

        part = pl.ds(pl.multiple_of(c * half, half), half)
        gated, slope = silu_and_slope(mm(r.n2s[j, part], r.upv[...]) + flat_row(r.upb))
        act = gated.astype(BF16)
        r.big[pl.ds(pl.multiple_of(j * rows + c * half, half), half)] = act
        pug = (mm_nt(r.ogs[j, part], r.downv[...]) * slope).astype(BF16)
        r.pug[j, part] = pug
        r.terms[j, part] = mm_nt(pug, r.upv[...]).astype(BF16)
        r.fterms[j, part] = mm(act, r.downv[...]).astype(BF16)

        for c in range(2):

            @pl.when(u == 2 * c + 1)
            def _(c=c):
                moves[f"t3{c}"].start()

            @pl.when(u == 2 * c + 2)
            def _(c=c):
                moves[f"t3{c}"].wait_recv()
                part = cut(c)
                r.crossb[part] = add_low(r.terms[2, part], r.near3[part])
                moves[f"c{c}"].start()

        @pl.when(u == 7)
        def _():
            moves["t1"].start()

        return carry

    lax.fori_loop(0, 8, ffn_step, 0)
    flat = (slabs * rows, width)
    r.acc[...] = mm_tn(r.ogs[...].reshape(flat), r.big[0 : slabs * rows])
    store_shards(r.dboth, r.acc)
    down_first.start()
    stores = [
        pltpu.make_async_copy(r.fterms, r.f_o, r.store.at[5]),
        pltpu.make_async_copy(r.res, r.res_o, r.store.at[6]),
    ]
    for copy in stores:
        copy.start()
    cot = r.ogs[0].astype(F32)
    r.sums[2:3] = jnp.sum(cot, 0, keepdims=True)
    moves["t1"].wait_recv()
    moves["c0"].wait_recv()
    moves["c1"].wait_recv()

    grad = r.terms[0].astype(F32) + r.near1[...].astype(F32) + r.crossr[...].astype(F32)
    scaled, inv_std = standardize(r.res[...])
    res_grad = cot + norm_back(grad, scaled, inv_std, flat_row(r.gain2))
    r.rg_o[...] = res_grad
    r.low[...] = res_grad.astype(BF16)
    r.sums[0:1] = jnp.sum(grad * scaled, 0, keepdims=True)
    r.sums[1:2] = jnp.sum(grad, 0, keepdims=True)
    r.mgt[...] = mm_nt(r.owv[...], r.low[...]).astype(BF16)
    for j in (2, 3, 1):
        moves[f"g{j}"].start()
        r.mgts[0] = r.mgt[my_rows]
    mixed = r.attt[0]
    r.acc[...] = mm(mixed, r.low[...])
    span = width // 2
    mine = pl.ds(pl.multiple_of(me % 2 * span, BLOCK), span)
    theirs = pl.ds(pl.multiple_of((1 - me % 2) * span, BLOCK), span)
    r.osent[...] = r.acc[:, theirs].astype(BF16)
    columns.start()
    r.ohalf[...] = r.acc[:, mine]
    r.acc[...] = mm_tn(r.n2s[...].reshape(flat), r.pug[...].reshape(flat))
    store_shards(r.uboth, r.acc)
    r.upb_sum[...] = jnp.sum(r.pug[...].reshape(flat).astype(F32), 0, keepdims=True)
    columns.wait_recv()
    r.ohalf[...] += r.ogot[...].astype(F32)
    store_shards(r.oboth, r.ohalf)
    more = [
        pltpu.make_async_copy(r.uboth, r.up_o, r.store.at[4]),
        pltpu.make_async_copy(r.oboth, r.ow_o, r.store.at[7]),
    ]
    for copy in more:
        copy.start()
    stores += more
    for j in range(1, slabs):
        moves[f"g{j}"].wait_recv()
    stores.append(pltpu.make_async_copy(r.mgts, r.mgt_o, r.store.at[8]))
    stores[-1].start()
    down_first.wait_recv()
    add_got(r.dboth.at[0], r.dgot)
    stores.append(pltpu.make_async_copy(r.dboth.at[0], r.down_o, r.store.at[9]))
    stores[-1].start()
    for copy in stores:
        copy.wait()
    total = slabs * heads
    for turn in (total - 2, total - 1):
        for copy in spills(turn // heads, turn % heads, turn % 2):
            copy.wait()
    for move in w.all:
        if move is not sent:
            move.wait_send()


def front(lens, x, og, gain1, bias1, gain2, bias2, upb, f1b, f2b, vw, f1, f2, ow, up, down):
    rows, width = x.shape
    heads, _, longest = f2.shape
    depth = vw.shape[1]
    units = up.shape[1]
    slabs = lax.axis_size("head")
    osh = shard_shape(width, width // 2)
    dsh = shard_shape(width, units)
    group = (slabs, rows, width)
    anywhere = pl.BlockSpec(memory_space=pl.ANY)
    vmem = pl.BlockSpec(memory_space=pltpu.VMEM)
    low = lambda *s: jax.ShapeDtypeStruct(s, BF16)
    wide = lambda *s: jax.ShapeDtypeStruct(s, F32)
    out_shape = [
        low(*group),
        low(slabs, width, rows),
        low(slabs, heads, rows, width),
        low(slabs, heads, rows, width),
        low(slabs, heads, rows, longest),
        low(slabs, depth, rows),
        low(slabs, depth, rows),
        low(*group),
        wide(rows, width),
        wide(rows, width),
        jax.ShapeDtypeStruct(dsh.shape[1:], BF16),
        dsh,
        osh,
        wide(1, units),
        wide(3, width),
    ]
    out_specs = [vmem if n in ("rg_o", "upb_sum", "sums") else anywhere for n in FRONT_OUT]
    vl = lambda *s: pltpu.VMEM(s, BF16)
    vf = lambda *s: pltpu.VMEM(s, F32)
    scratch = dict(
        xs=vl(*group),
        n1=vl(rows, width),
        n1t=vl(slabs, width, rows),
        big=vl(max(heads * width, slabs * rows), width),
        f2v=vl(heads, width, longest),
        hidb=vl(2, rows, width),
        slopeb=vl(2, rows, width),
        probb=vl(2, rows, longest),
        valt=vl(slabs, depth, rows),
        vwv=vl(width, depth),
        attt=vl(slabs, width, rows),
        owv=vl(width, width),
        upv=vl(width, units),
        downv=vl(units, width),
        ogs=vl(*group),
        n2s=vl(*group),
        pug=vl(slabs, rows, units),
        near1=vl(rows, width),
        near3=vl(rows, width),
        crossb=vl(rows, width),
        crossr=vl(rows, width),
        fterms=vl(*group),
        res=vf(rows, width),
        mgts=vl(slabs, depth, rows),
        acc=vf(width, width),
        vt=vl(depth, width),
        ohalf=vf(width, width // 2),
        osent=vl(width, width // 2),
        ogot=vl(width, width // 2),
        dboth=vl(*dsh.shape),
        dgot=vl(*dsh.shape[1:]),
        uboth=vl(*dsh.shape),
        oboth=vl(*osh.shape),
        send=pltpu.SemaphoreType.DMA((12 + 4 * slabs,)),
        recv=pltpu.SemaphoreType.DMA((12 + 4 * slabs,)),
        load=pltpu.SemaphoreType.DMA((6 + 2 * heads,)),
        spill=pltpu.SemaphoreType.DMA((2, 3)),
        store=pltpu.SemaphoreType.DMA((10,)),
    )
    smem = pl.BlockSpec(memory_space=pltpu.SMEM)
    return pl.pallas_call(
        front_kernel,
        out_shape=out_shape,
        in_specs=[smem] + [anywhere] * 2 + [vmem] * 7 + [anywhere] * 6,
        out_specs=out_specs,
        scratch_shapes=[scratch[n] for n in FRONT_SCRATCH],
        compiler_params=pltpu.CompilerParams(
            collective_id=0, has_side_effects=True, vmem_limit_bytes=FUSED_LIMIT
        ),
        cost_estimate=cost(
            slabs * rows * width * (heads * (width + longest) + 6 * units), 60 << 20
        ),
        name="front",
    )(lens, x, og, gain1, bias1, gain2, bias2, upb, f1b, f2b, vw, f1, f2, ow, up, down)


BACK_IN = (
    "lens", "upb_sum", "sums", "gain1", "downb", "vw", "hid", "slope", "prob", "n1t", "valt", "mgt",
    "f1", "f2", "xs", "fterms", "down", "up", "ow", "res", "rg",
)
BACK_OUT = ("result", "input", "ow_o", "down_o", "up_o", "f1_o", "f2_o", "val_o", "small_o")
BACK_SCRATCH = (
    "n1tv", "valtv", "mgtv", "vgt", "f1v", "f2v", "vtv", "terms", "probb", "sg", "pog",
    "acc1", "acc2", "acc3", "xb", "near3", "crossb", "near1", "crossr", "fb", "fnear3",
    "fnear1", "fcrossr", "resv", "rgv", "dk", "uk", "ugot", "ok", "ogot", "oall", "olow", "aboth",
    "agot", "bboth", "bgot", "vboth", "vgot", "small", "small_y", "small_z", "send",
    "recv", "load", "fetch", "store",
)


def back_kernel(*refs):
    r = types.SimpleNamespace(**dict(zip(BACK_IN + BACK_OUT + BACK_SCRATCH, refs)))
    slabs, heads, rows, width = r.pog.shape
    longest = r.probb.shape[2]
    depth = r.vgt.shape[1]
    dim = depth // heads
    blocks = rows // BLOCK
    count = r.ok.shape[0]
    me = lax.axis_index("head")
    turns = slabs * heads
    w = Wires(r.send, r.recv)
    up_group = Shards(w, r.uk, r.up.at[1], r.ugot, r.up_o, r.store.at[4 + 2 * heads])
    out_group = Shards(w, r.ok, r.ow.at[1], r.ogot, r.oall, r.store.at[0])
    out_heads = [w.remote(r.olow, r.ow_o.at[j], "head", j) for j in range(1, slabs)]
    down_rest = [w.remote(r.dk.at[k], r.down_o.at[k], "dp", 2 * k) for k in range(1, count)]
    f1_group, f2_group = [], []
    for h in range(heads):
        both, sem = r.bboth.at[h], r.store.at[1 + heads + h]
        f2_group.append(Shards(w, both.at[0], both.at[1], r.bgot.at[h], r.f2_o.at[h], sem))
        both, sem = r.aboth.at[h], r.store.at[1 + h]
        f1_group.append(Shards(w, both.at[0], both.at[1], r.agot.at[h], r.f1_o.at[h], sem))
    sem = r.store.at[1 + 2 * heads]
    val_group = Shards(w, r.vboth.at[0], r.vboth.at[1], r.vgot, r.val_o, sem)
    fterm1 = w.remote(r.fterms.at[1], r.fnear1, "head", 1)
    fterm3 = w.remote(r.fterms.at[3], r.fnear3, "head", 1)
    fcross = w.remote(r.fb, r.fcrossr, "head", 2)
    term1 = w.remote(r.terms.at[1], r.near1, "head", 1)
    term3 = w.remote(r.terms.at[3], r.near3, "head", 1)
    cross = w.remote(r.crossb, r.crossr, "head", 2)
    small_y = w.remote(r.small, r.small_y, "dp", 1)
    small_z = [
        w.remote(r.small_z.at[0], r.small_z.at[k], "dp", 2 * k) for k in range(1, count)
    ]
    small_x = [
        w.remote(r.small, r.small_o.at[j], "head", j) for j in range(1, slabs)
    ]
    own_low = pltpu.make_async_copy(r.olow, r.ow_o.at[0], r.store.at[2 + 2 * heads])
    own_down = pltpu.make_async_copy(r.dk.at[0], r.down_o.at[0], r.store.at[7 + 2 * heads])
    own_small = pltpu.make_async_copy(r.small, r.small_o.at[0], r.store.at[3 + 2 * heads])

    def load(index, src, dst):
        return pltpu.make_async_copy(src, dst, r.load.at[index])

    loads = [
        load(0, r.mgt, r.mgtv),
        load(1, r.valt, r.valtv),
        load(2, r.f2, r.f2v),
        load(3, r.n1t, r.n1tv),
        load(4, r.down, r.dk),
        load(5, r.fterms.at[2], r.fb),
        load(6, r.f1, r.f1v),
        load(7, r.xs.at[3], r.xb),
        load(8, r.res, r.resv),
        load(9, r.rg, r.rgv),
        load(10, r.up.at[0], r.uk),
        load(11, r.ow.at[0], r.ok),
    ]

    def fetches(turn):
        h, j, slot = turn // slabs, turn % slabs, turn % 2
        return [
            pltpu.make_async_copy(r.prob.at[j, h], r.probb.at[slot], r.fetch.at[slot, 0]),
            pltpu.make_async_copy(r.slope.at[j, h], r.terms.at[2 + slot], r.fetch.at[slot, 1]),
            pltpu.make_async_copy(r.hid.at[j, h], r.terms.at[slot], r.fetch.at[slot, 2]),
        ]

    for copy in loads[:2] + fetches(0) + loads[2:]:
        copy.start()
    r.vtv[...] = r.vw[...].T
    greet(partners())
    up_group.start()
    out_group.start()
    fterm3.start()
    fterm1.start()
    r.small[...] = jnp.zeros_like(r.small)
    r.small[2 * heads : 2 * heads + 1] = r.upb_sum[...]
    r.small[2 * heads + 3 : 2 * heads + 6] = r.sums[...]
    for copy in loads[:6]:
        copy.wait()
    for move in down_rest:
        move.start()
    own_down.start()

    def turn_step(turn, carry):
        h, j, slot = turn // slabs, turn % slabs, turn % 2
        for copy in fetches(turn):
            copy.wait()

        @pl.when(turn + 1 < turns)
        def _():
            for copy in fetches(turn + 1):
                copy.start()

        @pl.when(j == 0)
        def _():
            r.acc1[...] = jnp.zeros_like(r.acc1)
            r.acc2[...] = jnp.zeros_like(r.acc2)

        head_rows = pl.ds(pl.multiple_of(h * dim, dim), dim)
        mgt = r.mgtv[j, head_rows]
        r.vgt[j, head_rows] = mm(mgt, r.probb[slot]).astype(BF16)
        probs_grad = mm_tn(mgt, r.valtv[j, head_rows])
        first = jnp.bitwise_xor(me, j) * blocks
        zero = jnp.zeros((BLOCK, BLOCK), F32)
        for b in range(blocks):
            length = r.lens[first + b]
            own = slice(b * BLOCK, (b + 1) * BLOCK)
            prob = r.probb[slot, own].astype(F32)
            grad = probs_grad[own]
            inner = jnp.sum(prob * grad, -1, keepdims=True)
            parts = cells(prob * (grad - inner))
            is_full = length == longest
            is_half = length == longest // 2
            for c in range(blocks):
                half = parts[2 * (b // 2) + c] if c < 2 else zero
                quarter = parts[b] if c == 0 else zero
                cell = jnp.where(is_full, parts[c], jnp.where(is_half, half, quarter))
                r.sg[own, c * BLOCK : (c + 1) * BLOCK] = cell.astype(BF16)
        scores_grad = r.sg[...]
        row = pl.ds(h, 1)
        pog = (mm_nt(scores_grad, r.f2v[h]) * r.terms[2 + slot].astype(F32)).astype(BF16)
        r.pog[j, h] = pog
        r.small[row] += jnp.sum(pog.astype(F32), 0, keepdims=True)
        row = pl.ds(heads + h, 1)
        r.small[row, 0:longest] += jnp.sum(scores_grad.astype(F32), 0, keepdims=True)
        r.acc2[...] += mm_tn(r.terms[slot], scores_grad)
        r.acc1[...] += mm(r.n1tv[j], pog)

        for k in range(heads):

            @pl.when(turn == slabs * k + slabs - 1)
            def _(k=k):
                store_shards(r.bboth.at[k], r.acc2)
                f2_group[k].start()
                store_shards(r.aboth.at[k], r.acc1)
                f1_group[k].start()

        @pl.when(turn == 1)
        def _():
            fterm3.wait_recv()
            r.fb[...] = add_low(r.fb[...], r.fnear3[...])
            fcross.start()

        @pl.when(turn == slabs)
        def _():
            for copy in loads[10:]:
                copy.wait()
            up_group.second()

        @pl.when(turn == slabs + 2)
        def _():
            out_group.second()

        @pl.when(turn == 2 * slabs)
        def _():
            out_group.finish()
            r.olow[...] = sum(r.oall[k].astype(F32) for k in range(count)).astype(BF16)
            for move in out_heads:
                move.start()
            own_low.start()
            f2_group[0].second()

        return carry

    lax.fori_loop(0, turns, turn_step, 0)
    f1_group[0].second()
    for copy in loads[6:8]:
        copy.wait()

    def term_step(i, carry):
        j = slabs - 1 - i

        @pl.when(i > 0)
        def _():
            load(7, r.xs.at[j], r.xb).wait()

        term = mm_tn(r.vgt[j], r.vtv[...])
        for h in range(heads):
            term += mm_nt(r.pog[j, h], r.f1v[h])
        low = term.astype(BF16)
        r.terms[j] = low
        wide = low.astype(F32)
        scaled, _ = standardize(r.xb[...].astype(F32))
        base = 2 * heads + 1
        r.small[base : base + 1] += jnp.sum(wide * scaled, 0, keepdims=True)
        r.small[base + 1 : base + 2] += jnp.sum(wide, 0, keepdims=True)

        @pl.when(i < slabs - 1)
        def _():
            load(7, r.xs.at[j - 1], r.xb).start()

        @pl.when(i == 0)
        def _():
            term3.start()

        @pl.when(i == 1)
        def _():
            term3.wait_recv()
            r.crossb[...] = add_low(r.terms[2], r.near3[...])
            cross.start()

        @pl.when(i == 2)
        def _():
            term1.start()
            f2_group[1].second()

        return carry

    lax.fori_loop(0, slabs, term_step, 0)
    small_y.start()
    total = mm_nt(r.n1tv[0], r.vgt[0])
    for j in range(1, slabs):
        total += mm_nt(r.n1tv[j], r.vgt[j])
    r.acc3[...] = total
    store_shards(r.vboth, r.acc3)
    val_group.start()
    fcross.wait_send()
    own_fterm = load(12, r.fterms.at[0], r.fb)
    own_fterm.start()
    for copy in loads[8:10] + [own_fterm]:
        copy.wait()
    fterm1.wait_recv()
    fcross.wait_recv()
    others = r.fnear1[...].astype(F32) + r.fcrossr[...].astype(F32)
    r.resv[...] += r.fb[...].astype(F32) + others + flat_row(r.downb)
    finals = [pltpu.make_async_copy(r.resv, r.result, r.store.at[5 + 2 * heads])]
    finals[0].start()
    f1_group[1].second()
    for h in range(2, heads - 1):
        f2_group[h].second()
        f1_group[h].second()
    term1.wait_recv()
    cross.wait_recv()
    grad = r.terms[0].astype(F32) + r.near1[...].astype(F32) + r.crossr[...].astype(F32)
    scaled, inv_std = standardize(r.xb[...].astype(F32))
    r.rgv[...] += norm_back(grad, scaled, inv_std, flat_row(r.gain1))
    finals.append(pltpu.make_async_copy(r.rgv, r.input, r.store.at[6 + 2 * heads]))
    finals[1].start()
    small_y.wait_recv()
    r.small_z[0] = r.small[...] + r.small_y[...]
    for move in small_z:
        move.start()
    f2_group[-1].second()
    for move in small_z:
        move.wait_recv()
    small_y.wait_send()
    r.small[...] = sum(r.small_z[k] for k in range(count))
    for move in small_x:
        move.start()
    own_small.start()
    f1_group[-1].second()
    val_group.second()
    for group in [up_group, val_group] + f1_group + f2_group:
        group.finish()
    for move in down_rest + out_heads + small_x:
        move.wait_recv()
    for copy in finals + [own_down, own_low, own_small]:
        copy.wait()
    for move in w.all:
        if move is not small_y and move is not fcross:
            move.wait_send()


def low_shape(*shape):
    return jax.ShapeDtypeStruct(shape, BF16)


def wide_shape(*shape):
    return jax.ShapeDtypeStruct(shape, F32)


def back(*args):
    hid, f2, vw, ow = args[6], args[13], args[5], args[18]
    slabs, heads, rows, width = hid.shape
    longest = f2.shape[2]
    depth = vw.shape[1]
    _, count, part, span = ow.shape
    small = (2 * heads + 6 + 7) // 8 * 8
    low, wide = low_shape, wide_shape
    out_shape = [
        wide(rows, width),
        wide(rows, width),
        low(slabs, part, span),
        low(count, part, width),
        low(count, part, width),
        low(heads, count, part, width),
        low(heads, count, part, longest),
        low(count, part, depth),
        wide(slabs, small, width),
    ]
    vl = lambda *s: pltpu.VMEM(s, BF16)
    vf = lambda *s: pltpu.VMEM(s, F32)
    moves = 2 * (slabs - 1) + 2 * (count - 1) + (2 * heads + 3) * count + 7
    scratch = dict(
        n1tv=vl(slabs, width, rows),
        valtv=vl(slabs, depth, rows),
        mgtv=vl(slabs, depth, rows),
        vgt=vl(slabs, depth, rows),
        f1v=vl(heads, width, width),
        f2v=vl(heads, width, longest),
        vtv=vl(depth, width),
        probb=vl(2, rows, longest),
        sg=vl(rows, longest),
        pog=vl(slabs, heads, rows, width),
        acc1=vf(width, width),
        acc2=vf(width, longest),
        acc3=vf(width, depth),
        xb=vl(rows, width),
        terms=vl(slabs, rows, width),
        near3=vl(rows, width),
        crossb=vl(rows, width),
        near1=vl(rows, width),
        crossr=vl(rows, width),
        fb=vl(rows, width),
        fnear3=vl(rows, width),
        fnear1=vl(rows, width),
        fcrossr=vl(rows, width),
        resv=vf(rows, width),
        rgv=vf(rows, width),
        ok=vl(count, part, span),
        ogot=vl(count, part, span),
        oall=vl(count, part, span),
        olow=vl(part, span),
        dk=vl(count, part, width),
        uk=vl(count, part, width),
        ugot=vl(count, part, width),
        aboth=vl(heads, 2, count, part, width),
        agot=vl(heads, count, part, width),
        bboth=vl(heads, 2, count, part, longest),
        bgot=vl(heads, count, part, longest),
        vboth=vl(2, count, part, depth),
        vgot=vl(count, part, depth),
        small=vf(small, width),
        small_y=vf(small, width),
        small_z=vf(count, small, width),
        send=pltpu.SemaphoreType.DMA((moves,)),
        recv=pltpu.SemaphoreType.DMA((moves,)),
        load=pltpu.SemaphoreType.DMA((13,)),
        fetch=pltpu.SemaphoreType.DMA((2, 3)),
        store=pltpu.SemaphoreType.DMA((8 + 2 * heads,)),
    )
    smem = pl.BlockSpec(memory_space=pltpu.SMEM)
    anywhere = pl.BlockSpec(memory_space=pl.ANY)
    vmem = pl.BlockSpec(memory_space=pltpu.VMEM)
    return pl.pallas_call(
        back_kernel,
        out_shape=out_shape,
        in_specs=[smem] + [vmem] * 5 + [anywhere] * 15,
        out_specs=[anywhere] * len(out_shape),
        scratch_shapes=[scratch[n] for n in BACK_SCRATCH],
        compiler_params=pltpu.CompilerParams(
            collective_id=1, has_side_effects=True, vmem_limit_bytes=FUSED_LIMIT
        ),
        cost_estimate=cost(slabs * rows * width * heads * (3 * width + 2 * longest), 60 << 20),
        name="back",
    )(*args)


def finish_kernel(*refs):
    result, inp, small, down, up, ow, f1, f2, val = refs[:9]
    (
        result_o, input_o, f1b_o, f2b_o, upb_o, down_o, up_o, ow_o, f1_o, f2_o, val_o,
    ) = refs[9:20]
    shared = refs[20:25]
    result_o[...] = result[...]
    input_o[...] = inp[...]
    slabs = small.shape[0]
    heads = f1.shape[0]
    longest = f2.shape[3]
    count = f1.shape[1]
    me = lax.axis_index("head")
    for j in range(slabs):
        owner = jnp.bitwise_xor(me, j)
        upb_o[pl.ds(owner, 1)] = small[j, 2 * heads : 2 * heads + 1]
        for h in range(heads):
            f1b_o[pl.ds(owner * heads + h, 1)] = small[j, h : h + 1]
            f2b_o[pl.ds(owner * heads + h, 1)] = small[j, heads + h : heads + h + 1, 0:longest]
    first = 2 * heads + 1
    for i, ref in enumerate(shared):
        ref[...] = sum(small[j, first + i] for j in range(slabs))
    span = ow.shape[2]
    mine = pl.ds(pl.multiple_of(me % 2 * span, BLOCK), span)
    theirs = pl.ds(pl.multiple_of((1 - me % 2) * span, BLOCK), span)
    ow_o[:, mine] = sum(ow[j].astype(F32) for j in range(0, slabs, 2))
    ow_o[:, theirs] = sum(ow[j].astype(F32) for j in range(1, slabs, 2))
    total = lambda ref: sum(ref[k].astype(F32) for k in range(count))
    down_o[...] = total(down).T
    up_o[...] = total(up)
    val_o[...] = total(val)
    for h in range(heads):
        f1_o[h] = total(f1.at[h])
        f2_o[h] = total(f2.at[h])


def finish(members, *args):
    f1, f2, val = args[6:]
    rows, width = args[0].shape
    heads, _, part, longest = f2.shape
    wide = wide_shape
    return pl.pallas_call(
        finish_kernel,
        out_shape=[
            wide(rows, width),
            wide(rows, width),
            wide(members * heads, width),
            wide(members * heads, longest),
            wide(members, width),
            wide(width, part),
            wide(part, width),
            wide(part, width),
            wide(heads, part, width),
            wide(heads, part, longest),
            wide(part, val.shape[2]),
        ]
        + [wide(width)] * 5,
        compiler_params=pltpu.CompilerParams(vmem_limit_bytes=FUSED_LIMIT),
        cost_estimate=cost(0, 20 << 20),
        name="finish",
    )(*args)


def local(
    tokens,
    seq_len,
    norm1_gain,
    norm1_bias,
    f1_weight,
    f1_bias,
    f2_weight,
    f2_bias,
    value_weight,
    out_weight,
    norm2_gain,
    norm2_bias,
    up_weight,
    up_bias,
    down_weight,
    down_bias,
    out_grad,
):
    members = lax.axis_size("head")
    (
        xs, n1t, hid, slope, prob, valt, mgt, fterms, res_grad, residual, down_y, up_y, ow_y, upb,
        sums2,
    ) = front(
        seq_len, tokens, out_grad, norm1_gain, norm1_bias, norm2_gain, norm2_bias, up_bias, f1_bias,
        f2_bias, value_weight, f1_weight, f2_weight, out_weight, up_weight, down_weight,
    )
    (
        result, input_grad, ow_parts, down_parts, up_parts, f1_parts, f2_parts, val_parts, small,
    ) = back(
        seq_len, upb, sums2, norm1_gain, down_bias, value_weight, hid, slope, prob, n1t, valt, mgt,
        f1_weight, f2_weight, xs, fterms, down_y, up_y, ow_y, residual, res_grad,
    )
    (
        result, input_grad, f1b_all, f2b_all, upb_all, down_piece, up_piece, out_piece, f1_piece,
        f2_piece, value_piece, gain1_g, bias1_g, gain2_g, bias2_g, downb_g,
    ) = finish(
        members, result, input_grad, small, down_parts, up_parts, ow_parts, f1_parts, f2_parts,
        val_parts,
    )
    return (
        result,
        input_grad,
        gain1_g,
        bias1_g,
        f1_piece,
        f1b_all,
        f2_piece,
        f2b_all,
        value_piece,
        out_piece,
        gain2_g,
        bias2_g,
        up_piece,
        upb_all.reshape(-1),
        down_piece,
        downb_g,
    )


def solution(mesh):
    placed = (
        P(("dp", "head"), None),
        P("dp"),
        P(),
        P(),
        P("head", None, None),
        P("head", None),
        P("head", None, None),
        P("head", None),
        P(None, "head"),
        P(),
        P(),
        P(),
        P(None, "head"),
        P("head"),
        P("head", None),
        P(),
        P(("dp", "head"), None),
    )
    return jax.shard_map(
        local,
        mesh=mesh,
        in_specs=placed,
        out_specs=(
            P(("dp", "head"), None),
            P(("dp", "head"), None),
            P(),
            P(),
            P("head", "dp", None),
            P(),
            P("head", "dp", None),
            P(),
            P("dp", "head"),
            P("dp", None),
            P(),
            P(),
            P("dp", "head"),
            P(),
            P("head", "dp"),
            P(),
        ),
        check_vma=False,
    )
```

time: 259 us -> 225 us (0.87)
  Pallas kernels: 237 us -> 219 us
  local copies, waits for them, and re-layouts: 13.3 us -> 5.06 us
  waiting for transfers between devices: 5.47 us -> 0 us
    pallas_call x1, Pallas kernels: 120 us -> 89.8 us  [front(): pl.pallas_call(front_kernel, out_shape=out_shape, in_specs=[smem] + [anyw...]
    pallas_call x1, Pallas kernels: 109 us -> 123 us  [back(): pl.pallas_call(back_kernel, out_shape=out_shape, in_specs=[smem] + [vmem]...]
    ppermute x2 -> x0, waiting for transfers between devices: 5.47 us -> none  [swap(): lax.ppermute(value, axis, [(i, i ^ step) for i in range(lax.axis_size(axi...]
    another operation x7 -> x0, local copies, waits for them, and re-layouts: 4.77 us -> none  [local(): jnp.stack([norm1_gain, norm1_bias, norm2_gain, norm2_bias, up_bias, down_...]
    unnamed x14 -> x2, local copies, waits for them, and re-layouts: 5.18 us -> 3.75 us
  transfers between devices with their start and end apart: 2 -> 0, of which waited for: 2 -> 0; matrix products, arithmetic and copies ran while one was open for 0% -> 0% of each run, Pallas kernels for 0% -> 0%
where the time goes in v1:
time: 225 us; the launch traced here: 224 us
  Pallas kernels  219 us (97%)
  local copies, waits for them, and re-layouts  5.06 us (2%)
    pallas_call x1, Pallas kernels, back(): pl.pallas_call(back_kernel, out_shape=out_shape, in_specs=[smem] + [vmem]...  123 us
    pallas_call x1, Pallas kernels, front(): pl.pallas_call(front_kernel, out_shape=out_shape, in_specs=[smem] + [anyw...  89.8 us
    pallas_call x1, Pallas kernels, finish(): pl.pallas_call(finish_kernel, out_shape=[wide(rows, width), wide(rows, wi...  6.02 us

profile of v1, /device:TPU:0, one launch (start us, length us, event | category | flops | bytes accessed | tf_op | source)
XLA Modules:
  0.0 224.3 jit_solution(7573742536899847101)
XLA Ops:
  0.6 1.9 copy.33.refs_10_.refs_5_
  2.5 89.8 %front.1 = (bf16[4,512,768]{2,1,0:T(8,128)(2,1)}, bf16[4,768,512]{2,1,0:T(8,128)(2,1)}, bf16[4,3,512,768]{3,2,1,0:T(8,128)(2,1)}, bf16[4,3,512,768]{3,2,1,0:T(8,...) custom-call(s32[16]{0:T(128)} %refs_0_.3, ...), custom_call_target="tpu_custom_call" | custom-call | flops 26575110144 | bytes 62914560 | tf_op jit(solution)/shard_map/front/pallas_call | solution.py:560
  92.3 122.7 %back.1 = (f32[512,768]{1,0:T(8,128)}, f32[512,768]{1,0:T(8,128)}, bf16[4,96,384]{2,1,0:T(8,128)(2,1)}, bf16[4,96,768]{2,1,0:T(8,128)(2,1)}, bf16[4,96,768]{2,1,...) custom-call(s32[16]{0:T(128)} %refs_0_.3, ...), custom_call_target="tpu_custom_call" | custom-call | flops 31406948352 | bytes 62914560 | tf_op jit(solution)/shard_map/back/pallas_call | solution.py:934
  215.1 6.0 %finish.1 = (f32[512,768]{1,0:T(8,128)}, f32[512,768]{1,0:T(8,128)}, f32[12,768]{1,0:T(8,128)}, f32[12,512]{1,0:T(8,128)}, f32[4,768]{1,0:T(4,128)}, /*index=5*/...) custom-call(f32[512,768]{1,0:T(8,128)} %get-tuple-element.71.refs_0_, ...), custom_call_target="tpu_custom_call" | custom-call | bytes 20971520 | tf_op jit(solution)/shard_map/finish/pallas_call | solution.py:989
  221.1 1.3 reshape.35
  222.4 1.9 copy.35

commit v2 on v1

--- a/solution.py
+++ b/solution.py
@@ -57,7 +57,12 @@
     me = lax.axis_index("dp")
     for d in range(2 * count):
         side = jnp.bitwise_xor(me % 2, d % 2)
-        place = jnp.bitwise_xor(me // 2, d // 2)
+        other = jnp.bitwise_xor(me // 2, d // 2)
+        gray = jnp.bitwise_xor(other, other // 2)
+        place, size, bit = 0, count // 2, 1
+        while size:
+            place = place + gray // bit % 2 * size
+            size, bit = size // 2, bit * 2
         both[side, place] = acc[d * depth : (d + 1) * depth].astype(BF16)
 
 
@@ -86,28 +91,55 @@
         return move
 
 
+def masks(count):
+    found = [1]
+    while 2 ** (len(found) + 1) <= count:
+        found.append(2 * found[-1] + 1)
+    return found
+
+
 class Shards:
-    def __init__(self, wires, keep, send, got, out, local_sem):
-        self.keep, self.got = keep, got
+    def __init__(self, wires, keep, send, got, out, own_sem, load_sem):
+        self.keep, self.got, self.out, self.load_sem = keep, got, out, load_sem
         self.count = keep.shape[0]
-        self.first = wires.remote(send, got, "dp", 1)
-        self.rest = [
-            wires.remote(keep.at[k], out.at[k], "dp", 2 * k) for k in range(1, self.count)
-        ]
-        self.own = pltpu.make_async_copy(keep.at[0], out.at[0], local_sem)
+        self.first = None if send is None else wires.remote(send, got, "dp", 1)
+        self.steps = []
+        size = self.count
+        for mask in masks(self.count):
+            size //= 2
+            part = pl.ds(size, size)
+            move = wires.remote(keep.at[part], out.at[part], "dp", 2 * mask)
+            self.steps.append((size, move))
+        self.own = pltpu.make_async_copy(keep.at[0], out.at[0], own_sem)
 
     def start(self):
         self.first.start()
 
+    def add(self, size):
+        for k in range(size):
+            self.keep[k] = add_low(self.keep[k], self.got[k])
+
     def second(self):
-        self.first.wait_recv()
-        for k in list(range(1, self.count)) + [0]:
-            self.keep[k] = add_low(self.keep[k], self.got[k])
-            (self.rest[k - 1] if k else self.own).start()
+        if self.first is not None:
+            self.first.wait_recv()
+            self.add(self.count)
+        self.steps[0][1].start()
+
+    def third(self):
+        for (size, move), (_, after) in zip(self.steps, self.steps[1:]):
+            move.wait_recv()
+            part = pl.ds(0, size)
+            copy = pltpu.make_async_copy(
+                self.out.at[pl.ds(size, size)], self.got.at[part], self.load_sem
+            )
+            copy.start()
+            copy.wait()
+            self.add(size)
+            after.start()
+        self.own.start()
 
     def finish(self):
-        for move in self.rest:
-            move.wait_recv()
+        self.steps[-1][1].wait_recv()
         self.own.wait()
 
 
@@ -128,13 +160,13 @@
     pl.semaphore_wait(barrier, len(axes))
 
 
-def partners():
-    over_dp = [1] + list(range(2, lax.axis_size("dp"), 2))
+def partners(far):
+    over_dp = [1] + [2 * mask for mask in masks(lax.axis_size("dp") // 2) if far]
     return [("head", s) for s in range(1, lax.axis_size("head"))] + [("dp", s) for s in over_dp]
 
 
 FRONT_IN = (
-    "lens", "x", "og", "gain1", "bias1", "gain2", "bias2", "upb", "f1b", "f2b", "vw", "f1", "f2",
+    "lens", "x", "og", "gain1", "bias1", "gain2", "bias2", "upb", "f1b", "f2b", "vt", "f1", "f2",
     "ow", "up", "down",
 )
 FRONT_OUT = (
@@ -142,9 +174,9 @@
     "down_o", "up_o", "ow_o", "upb_sum", "sums",
 )
 FRONT_SCRATCH = (
-    "xs", "n1", "n1t", "big", "f2v", "vwv", "hidb", "slopeb", "probb", "valt", "attt", "owv", "upv",
+    "xs", "n1", "n1t", "big", "f2v", "hidb", "slopeb", "probb", "valt", "attt", "owv", "upv",
     "downv", "ogs", "n2s", "pug", "near1", "near3", "crossb", "crossr", "fterms", "res", "mgts",
-    "acc", "vt", "ohalf", "osent", "ogot", "dboth", "dgot", "uboth", "oboth", "send", "recv",
+    "acc", "ohalf", "osent", "ogot", "dboth", "dgot", "uboth", "oboth", "send", "recv",
     "load", "spill", "store",
 )
 
@@ -231,17 +263,13 @@
         pltpu.make_async_copy(r.down, r.downv, r.load.at[base + 2]),
         pltpu.make_async_copy(r.og, r.ogs.at[0], r.load.at[base + 3]),
     ]
-    columns_load = pltpu.make_async_copy(r.vw, r.vwv, r.load.at[base + 4])
-    columns_load.start()
     for copy in loads:
         copy.start()
-    greet(partners())
+    greet(partners(False))
     moves["x2"].start()
     moves["x1"].start()
     for copy in late:
         copy.start()
-    columns_load.wait()
-    r.vt[...] = r.vwv[...].T
     loads[0].wait()
 
     def spills(j, h, slot):
@@ -483,10 +511,10 @@
             move.wait_send()
 
 
-def front(lens, x, og, gain1, bias1, gain2, bias2, upb, f1b, f2b, vw, f1, f2, ow, up, down):
+def front(lens, x, og, gain1, bias1, gain2, bias2, upb, f1b, f2b, vt, f1, f2, ow, up, down):
     rows, width = x.shape
     heads, _, longest = f2.shape
-    depth = vw.shape[1]
+    depth = vt.shape[0]
     units = up.shape[1]
     slabs = lax.axis_size("head")
     osh = shard_shape(width, width // 2)
@@ -526,7 +554,6 @@
         slopeb=vl(2, rows, width),
         probb=vl(2, rows, longest),
         valt=vl(slabs, depth, rows),
-        vwv=vl(width, depth),
         attt=vl(slabs, width, rows),
         owv=vl(width, width),
         upv=vl(width, units),
@@ -542,7 +569,6 @@
         res=vf(rows, width),
         mgts=vl(slabs, depth, rows),
         acc=vf(width, width),
-        vt=vl(depth, width),
         ohalf=vf(width, width // 2),
         osent=vl(width, width // 2),
         ogot=vl(width, width // 2),
@@ -552,7 +578,7 @@
         oboth=vl(*osh.shape),
         send=pltpu.SemaphoreType.DMA((12 + 4 * slabs,)),
         recv=pltpu.SemaphoreType.DMA((12 + 4 * slabs,)),
-        load=pltpu.SemaphoreType.DMA((6 + 2 * heads,)),
+        load=pltpu.SemaphoreType.DMA((5 + 2 * heads,)),
         spill=pltpu.SemaphoreType.DMA((2, 3)),
         store=pltpu.SemaphoreType.DMA((10,)),
     )
@@ -560,7 +586,7 @@
     return pl.pallas_call(
         front_kernel,
         out_shape=out_shape,
-        in_specs=[smem] + [anywhere] * 2 + [vmem] * 7 + [anywhere] * 6,
+        in_specs=[smem] + [anywhere] * 2 + [vmem] * 8 + [anywhere] * 5,
         out_specs=out_specs,
         scratch_shapes=[scratch[n] for n in FRONT_SCRATCH],
         compiler_params=pltpu.CompilerParams(
@@ -570,25 +596,27 @@
             slabs * rows * width * (heads * (width + longest) + 6 * units), 60 << 20
         ),
         name="front",
-    )(lens, x, og, gain1, bias1, gain2, bias2, upb, f1b, f2b, vw, f1, f2, ow, up, down)
+    )(lens, x, og, gain1, bias1, gain2, bias2, upb, f1b, f2b, vt, f1, f2, ow, up, down)
 
 
 BACK_IN = (
-    "lens", "upb_sum", "sums", "gain1", "downb", "vw", "hid", "slope", "prob", "n1t", "valt", "mgt",
+    "lens", "upb_sum", "sums", "gain1", "downb", "vt", "hid", "slope", "prob", "n1t", "valt", "mgt",
     "f1", "f2", "xs", "fterms", "down", "up", "ow", "res", "rg",
 )
 BACK_OUT = ("result", "input", "ow_o", "down_o", "up_o", "f1_o", "f2_o", "val_o", "small_o")
 BACK_SCRATCH = (
-    "n1tv", "valtv", "mgtv", "vgt", "f1v", "f2v", "vtv", "terms", "probb", "sg", "pog",
-    "acc1", "acc2", "acc3", "xb", "near3", "crossb", "near1", "crossr", "fb", "fnear3",
-    "fnear1", "fcrossr", "resv", "rgv", "dk", "uk", "ugot", "ok", "ogot", "oall", "olow", "aboth",
-    "agot", "bboth", "bgot", "vboth", "vgot", "small", "small_y", "small_z", "send",
+    "n1tv", "valtv", "mgtv", "vgt", "f1v", "f2v", "terms", "probb", "sg", "pog",
+    "acc1", "acc2", "acc3", "xb", "near3", "near1", "crossr", "fb", "fnear3",
+    "fnear1", "fcrossr", "rgv", "dk", "dgot", "uk", "ugot", "ok", "ogot", "oall", "olow", "aboth",
+    "agot", "bboth", "bgot", "vboth", "vgot", "small", "small_in", "send",
     "recv", "load", "fetch", "store",
 )
 
 
 def back_kernel(*refs):
     r = types.SimpleNamespace(**dict(zip(BACK_IN + BACK_OUT + BACK_SCRATCH, refs)))
+    r.crossb = r.terms.at[3]
+    r.resv = r.acc1.at[pl.ds(0, r.rgv.shape[0])]
     slabs, heads, rows, width = r.pog.shape
     longest = r.probb.shape[2]
     depth = r.vgt.shape[1]
@@ -598,34 +626,39 @@
     me = lax.axis_index("head")
     turns = slabs * heads
     w = Wires(r.send, r.recv)
-    up_group = Shards(w, r.uk, r.up.at[1], r.ugot, r.up_o, r.store.at[4 + 2 * heads])
-    out_group = Shards(w, r.ok, r.ow.at[1], r.ogot, r.oall, r.store.at[0])
+    sems = iter(range(4 * heads + 8))
+
+    def shards(keep, send, got, out):
+        return Shards(w, keep, send, got, out, r.store.at[next(sems)], r.store.at[next(sems)])
+
+    down_group = shards(r.dk, None, r.dgot, r.down_o)
+    up_group = shards(r.uk, r.up.at[1], r.ugot, r.up_o)
+    out_group = shards(r.ok, r.ow.at[1], r.ogot, r.oall)
     out_heads = [w.remote(r.olow, r.ow_o.at[j], "head", j) for j in range(1, slabs)]
-    down_rest = [w.remote(r.dk.at[k], r.down_o.at[k], "dp", 2 * k) for k in range(1, count)]
     f1_group, f2_group = [], []
     for h in range(heads):
-        both, sem = r.bboth.at[h], r.store.at[1 + heads + h]
-        f2_group.append(Shards(w, both.at[0], both.at[1], r.bgot.at[h], r.f2_o.at[h], sem))
-        both, sem = r.aboth.at[h], r.store.at[1 + h]
-        f1_group.append(Shards(w, both.at[0], both.at[1], r.agot.at[h], r.f1_o.at[h], sem))
-    sem = r.store.at[1 + 2 * heads]
-    val_group = Shards(w, r.vboth.at[0], r.vboth.at[1], r.vgot, r.val_o, sem)
+        both = r.bboth.at[h]
+        f2_group.append(shards(both.at[0], both.at[1], r.bgot.at[h], r.f2_o.at[h]))
+        both = r.aboth.at[h]
+        f1_group.append(shards(both.at[0], both.at[1], r.agot.at[h], r.f1_o.at[h]))
+    val_group = shards(r.vboth.at[0], r.vboth.at[1], r.vgot, r.val_o)
     fterm1 = w.remote(r.fterms.at[1], r.fnear1, "head", 1)
     fterm3 = w.remote(r.fterms.at[3], r.fnear3, "head", 1)
     fcross = w.remote(r.fb, r.fcrossr, "head", 2)
     term1 = w.remote(r.terms.at[1], r.near1, "head", 1)
     term3 = w.remote(r.terms.at[3], r.near3, "head", 1)
     cross = w.remote(r.crossb, r.crossr, "head", 2)
-    small_y = w.remote(r.small, r.small_y, "dp", 1)
-    small_z = [
-        w.remote(r.small_z.at[0], r.small_z.at[k], "dp", 2 * k) for k in range(1, count)
+    steps = [1] + [2 * mask for mask in masks(count)]
+    small_steps = [
+        w.remote(r.small.at[i], r.small_in.at[i], "dp", step) for i, step in enumerate(steps)
     ]
+    small_last = r.small.at[len(steps)]
     small_x = [
-        w.remote(r.small, r.small_o.at[j], "head", j) for j in range(1, slabs)
+        w.remote(small_last, r.small_o.at[j], "head", j) for j in range(1, slabs)
     ]
-    own_low = pltpu.make_async_copy(r.olow, r.ow_o.at[0], r.store.at[2 + 2 * heads])
-    own_down = pltpu.make_async_copy(r.dk.at[0], r.down_o.at[0], r.store.at[7 + 2 * heads])
-    own_small = pltpu.make_async_copy(r.small, r.small_o.at[0], r.store.at[3 + 2 * heads])
+    base = 4 * heads + 8
+    own_low = pltpu.make_async_copy(r.olow, r.ow_o.at[0], r.store.at[base])
+    own_small = pltpu.make_async_copy(small_last, r.small_o.at[0], r.store.at[base + 1])
 
     def load(index, src, dst):
         return pltpu.make_async_copy(src, dst, r.load.at[index])
@@ -639,7 +672,6 @@
         load(5, r.fterms.at[2], r.fb),
         load(6, r.f1, r.f1v),
         load(7, r.xs.at[3], r.xb),
-        load(8, r.res, r.resv),
         load(9, r.rg, r.rgv),
         load(10, r.up.at[0], r.uk),
         load(11, r.ow.at[0], r.ok),
@@ -655,20 +687,17 @@
 
     for copy in loads[:2] + fetches(0) + loads[2:]:
         copy.start()
-    r.vtv[...] = r.vw[...].T
-    greet(partners())
+    greet(partners(True))
     up_group.start()
     out_group.start()
     fterm3.start()
     fterm1.start()
-    r.small[...] = jnp.zeros_like(r.small)
-    r.small[2 * heads : 2 * heads + 1] = r.upb_sum[...]
-    r.small[2 * heads + 3 : 2 * heads + 6] = r.sums[...]
+    r.small[0] = jnp.zeros(r.small.shape[1:], F32)
+    r.small[0, 2 * heads : 2 * heads + 1] = r.upb_sum[...]
+    r.small[0, 2 * heads + 3 : 2 * heads + 6] = r.sums[...]
     for copy in loads[:6]:
         copy.wait()
-    for move in down_rest:
-        move.start()
-    own_down.start()
+    down_group.second()
 
     def turn_step(turn, carry):
         h, j, slot = turn // slabs, turn % slabs, turn % 2
@@ -709,9 +738,9 @@
         row = pl.ds(h, 1)
         pog = (mm_nt(scores_grad, r.f2v[h]) * r.terms[2 + slot].astype(F32)).astype(BF16)
         r.pog[j, h] = pog
-        r.small[row] += jnp.sum(pog.astype(F32), 0, keepdims=True)
+        r.small[0, row] += jnp.sum(pog.astype(F32), 0, keepdims=True)
         row = pl.ds(heads + h, 1)
-        r.small[row, 0:longest] += jnp.sum(scores_grad.astype(F32), 0, keepdims=True)
+        r.small[0, row, 0:longest] += jnp.sum(scores_grad.astype(F32), 0, keepdims=True)
         r.acc2[...] += mm_tn(r.terms[slot], scores_grad)
         r.acc1[...] += mm(r.n1tv[j], pog)
 
@@ -722,7 +751,8 @@
                 store_shards(r.bboth.at[k], r.acc2)
                 f2_group[k].start()
                 store_shards(r.aboth.at[k], r.acc1)
-                f1_group[k].start()
+                if k < heads - 1:
+                    f1_group[k].start()
 
         @pl.when(turn == 1)
         def _():
@@ -730,24 +760,34 @@
             r.fb[...] = add_low(r.fb[...], r.fnear3[...])
             fcross.start()
 
+        @pl.when(turn == slabs - 1)
+        def _():
+            down_group.third()
+
         @pl.when(turn == slabs)
         def _():
-            for copy in loads[10:]:
+            for copy in loads[9:]:
                 copy.wait()
             up_group.second()
 
         @pl.when(turn == slabs + 2)
         def _():
             out_group.second()
+            up_group.third()
 
         @pl.when(turn == 2 * slabs)
         def _():
+            out_group.third()
+            f2_group[0].second()
+
+        @pl.when(turn == 2 * slabs + 2)
+        def _():
             out_group.finish()
-            r.olow[...] = sum(r.oall[k].astype(F32) for k in range(count)).astype(BF16)
+            r.olow[...] = (r.oall[0].astype(F32) + r.oall[1].astype(F32)).astype(BF16)
             for move in out_heads:
                 move.start()
             own_low.start()
-            f2_group[0].second()
+            f2_group[0].third()
 
         return carry
 
@@ -755,6 +795,8 @@
     f1_group[0].second()
     for copy in loads[6:8]:
         copy.wait()
+    res_load = load(8, r.res, r.resv)
+    res_load.start()
 
     def term_step(i, carry):
         j = slabs - 1 - i
@@ -763,16 +805,16 @@
         def _():
             load(7, r.xs.at[j], r.xb).wait()
 
-        term = mm_tn(r.vgt[j], r.vtv[...])
+        term = mm_tn(r.vgt[j], r.vt[...])
         for h in range(heads):
             term += mm_nt(r.pog[j, h], r.f1v[h])
         low = term.astype(BF16)
         r.terms[j] = low
         wide = low.astype(F32)
         scaled, _ = standardize(r.xb[...].astype(F32))
-        base = 2 * heads + 1
-        r.small[base : base + 1] += jnp.sum(wide * scaled, 0, keepdims=True)
-        r.small[base + 1 : base + 2] += jnp.sum(wide, 0, keepdims=True)
+        at = 2 * heads + 1
+        r.small[0, at : at + 1] += jnp.sum(wide * scaled, 0, keepdims=True)
+        r.small[0, at + 1 : at + 2] += jnp.sum(wide, 0, keepdims=True)
 
         @pl.when(i < slabs - 1)
         def _():
@@ -785,18 +827,24 @@
         @pl.when(i == 1)
         def _():
             term3.wait_recv()
+            term3.wait_send()
             r.crossb[...] = add_low(r.terms[2], r.near3[...])
             cross.start()
 
         @pl.when(i == 2)
         def _():
             term1.start()
+            f1_group[0].third()
+
+        @pl.when(i == 3)
+        def _():
             f2_group[1].second()
 
         return carry
 
     lax.fori_loop(0, slabs, term_step, 0)
-    small_y.start()
+    small_steps[0].start()
+    f1_group[-1].start()
     total = mm_nt(r.n1tv[0], r.vgt[0])
     for j in range(1, slabs):
         total += mm_nt(r.n1tv[j], r.vgt[j])
@@ -806,47 +854,43 @@
     fcross.wait_send()
     own_fterm = load(12, r.fterms.at[0], r.fb)
     own_fterm.start()
-    for copy in loads[8:10] + [own_fterm]:
+    for copy in [res_load, loads[8], own_fterm]:
         copy.wait()
     fterm1.wait_recv()
     fcross.wait_recv()
     others = r.fnear1[...].astype(F32) + r.fcrossr[...].astype(F32)
     r.resv[...] += r.fb[...].astype(F32) + others + flat_row(r.downb)
-    finals = [pltpu.make_async_copy(r.resv, r.result, r.store.at[5 + 2 * heads])]
+    finals = [pltpu.make_async_copy(r.resv, r.result, r.store.at[base + 2])]
     finals[0].start()
+    f2_group[1].third()
     f1_group[1].second()
-    for h in range(2, heads - 1):
-        f2_group[h].second()
-        f1_group[h].second()
     term1.wait_recv()
     cross.wait_recv()
     grad = r.terms[0].astype(F32) + r.near1[...].astype(F32) + r.crossr[...].astype(F32)
     scaled, inv_std = standardize(r.xb[...].astype(F32))
     r.rgv[...] += norm_back(grad, scaled, inv_std, flat_row(r.gain1))
-    finals.append(pltpu.make_async_copy(r.rgv, r.input, r.store.at[6 + 2 * heads]))
+    finals.append(pltpu.make_async_copy(r.rgv, r.input, r.store.at[base + 3]))
     finals[1].start()
-    small_y.wait_recv()
-    r.small_z[0] = r.small[...] + r.small_y[...]
-    for move in small_z:
-        move.start()
-    f2_group[-1].second()
-    for move in small_z:
+    f1_group[1].third()
+    f2_group[2].second()
+    for i, move in enumerate(small_steps):
         move.wait_recv()
-    small_y.wait_send()
-    r.small[...] = sum(r.small_z[k] for k in range(count))
-    for move in small_x:
-        move.start()
-    own_small.start()
-    f1_group[-1].second()
+        r.small[i + 1] = r.small[i] + r.small_in[i]
+        for after in small_steps[i + 1 : i + 2] or small_x + [own_small]:
+            after.start()
+    f2_group[2].third()
+    f1_group[2].second()
     val_group.second()
-    for group in [up_group, val_group] + f1_group + f2_group:
+    f1_group[2].third()
+    val_group.third()
+    for group in [down_group, up_group] + f2_group + f1_group + [val_group]:
         group.finish()
-    for move in down_rest + out_heads + small_x:
+    for move in out_heads + small_x:
         move.wait_recv()
-    for copy in finals + [own_down, own_low, own_small]:
+    for copy in finals + [own_low, own_small]:
         copy.wait()
     for move in w.all:
-        if move is not small_y and move is not fcross:
+        if move is not term3 and move is not fcross:
             move.wait_send()
 
 
@@ -859,10 +903,10 @@
 
 
 def back(*args):
-    hid, f2, vw, ow = args[6], args[13], args[5], args[18]
+    hid, f2, vt, ow = args[6], args[13], args[5], args[18]
     slabs, heads, rows, width = hid.shape
     longest = f2.shape[2]
-    depth = vw.shape[1]
+    depth = vt.shape[0]
     _, count, part, span = ow.shape
     small = (2 * heads + 6 + 7) // 8 * 8
     low, wide = low_shape, wide_shape
@@ -879,7 +923,8 @@
     ]
     vl = lambda *s: pltpu.VMEM(s, BF16)
     vf = lambda *s: pltpu.VMEM(s, F32)
-    moves = 2 * (slabs - 1) + 2 * (count - 1) + (2 * heads + 3) * count + 7
+    steps = len(masks(count)) + 1
+    moves = 2 * (slabs - 1) + (2 * heads + 5) * steps + 6
     scratch = dict(
         n1tv=vl(slabs, width, rows),
         valtv=vl(slabs, depth, rows),
@@ -887,7 +932,6 @@
         vgt=vl(slabs, depth, rows),
         f1v=vl(heads, width, width),
         f2v=vl(heads, width, longest),
-        vtv=vl(depth, width),
         probb=vl(2, rows, longest),
         sg=vl(rows, longest),
         pog=vl(slabs, heads, rows, width),
@@ -897,20 +941,19 @@
         xb=vl(rows, width),
         terms=vl(slabs, rows, width),
         near3=vl(rows, width),
-        crossb=vl(rows, width),
         near1=vl(rows, width),
         crossr=vl(rows, width),
         fb=vl(rows, width),
         fnear3=vl(rows, width),
         fnear1=vl(rows, width),
         fcrossr=vl(rows, width),
-        resv=vf(rows, width),
         rgv=vf(rows, width),
         ok=vl(count, part, span),
         ogot=vl(count, part, span),
         oall=vl(count, part, span),
         olow=vl(part, span),
         dk=vl(count, part, width),
+        dgot=vl(count // 2, part, width),
         uk=vl(count, part, width),
         ugot=vl(count, part, width),
         aboth=vl(heads, 2, count, part, width),
@@ -919,14 +962,13 @@
         bgot=vl(heads, count, part, longest),
         vboth=vl(2, count, part, depth),
         vgot=vl(count, part, depth),
-        small=vf(small, width),
-        small_y=vf(small, width),
-        small_z=vf(count, small, width),
+        small=vf(steps + 1, small, width),
+        small_in=vf(steps, small, width),
         send=pltpu.SemaphoreType.DMA((moves,)),
         recv=pltpu.SemaphoreType.DMA((moves,)),
         load=pltpu.SemaphoreType.DMA((13,)),
         fetch=pltpu.SemaphoreType.DMA((2, 3)),
-        store=pltpu.SemaphoreType.DMA((8 + 2 * heads,)),
+        store=pltpu.SemaphoreType.DMA((12 + 4 * heads,)),
     )
     smem = pl.BlockSpec(memory_space=pltpu.SMEM)
     anywhere = pl.BlockSpec(memory_space=pl.ANY)
@@ -956,11 +998,12 @@
     slabs = small.shape[0]
     heads = f1.shape[0]
     longest = f2.shape[3]
-    count = f1.shape[1]
     me = lax.axis_index("head")
     for j in range(slabs):
         owner = jnp.bitwise_xor(me, j)
-        upb_o[pl.ds(owner, 1)] = small[j, 2 * heads : 2 * heads + 1]
+        units = small.shape[2]
+        own = small[owner, 2 * heads : 2 * heads + 1]
+        upb_o[j * units : (j + 1) * units] = own.reshape(units)
         for h in range(heads):
             f1b_o[pl.ds(owner * heads + h, 1)] = small[j, h : h + 1]
             f2b_o[pl.ds(owner * heads + h, 1)] = small[j, heads + h : heads + h + 1, 0:longest]
@@ -972,8 +1015,8 @@
     theirs = pl.ds(pl.multiple_of((1 - me % 2) * span, BLOCK), span)
     ow_o[:, mine] = sum(ow[j].astype(F32) for j in range(0, slabs, 2))
     ow_o[:, theirs] = sum(ow[j].astype(F32) for j in range(1, slabs, 2))
-    total = lambda ref: sum(ref[k].astype(F32) for k in range(count))
-    down_o[...] = total(down).T
+    total = lambda ref: ref[0].astype(F32) + ref[1].astype(F32)
+    down_o[...] = total(down)
     up_o[...] = total(up)
     val_o[...] = total(val)
     for h in range(heads):
@@ -986,22 +1029,29 @@
     rows, width = args[0].shape
     heads, _, part, longest = f2.shape
     wide = wide_shape
+    out_shape = [
+        wide(rows, width),
+        wide(rows, width),
+        wide(members * heads, width),
+        wide(members * heads, longest),
+        wide(members * width),
+        wide(part, width),
+        wide(part, width),
+        wide(part, width),
+        wide(heads, part, width),
+        wide(heads, part, longest),
+        wide(part, val.shape[2]),
+    ] + [wide(width)] * 5
+    whole = lambda v: pl.BlockSpec(v.shape, lambda _: (0,) * v.ndim)
+    pair = lambda v: pl.BlockSpec((2,) + v.shape[1:], lambda _: (0, 0, 0))
+    heads_pair = lambda v: pl.BlockSpec((heads, 2) + v.shape[2:], lambda _: (0, 0, 0, 0))
+    kinds = [whole] * 3 + [pair] * 2 + [whole] + [heads_pair] * 2 + [pair]
     return pl.pallas_call(
         finish_kernel,
-        out_shape=[
-            wide(rows, width),
-            wide(rows, width),
-            wide(members * heads, width),
-            wide(members * heads, longest),
-            wide(members, width),
-            wide(width, part),
-            wide(part, width),
-            wide(part, width),
-            wide(heads, part, width),
-            wide(heads, part, longest),
-            wide(part, val.shape[2]),
-        ]
-        + [wide(width)] * 5,
+        grid=(1,),
+        out_shape=out_shape,
+        in_specs=[kind(v) for kind, v in zip(kinds, args)],
+        out_specs=[whole(v) for v in out_shape],
         compiler_params=pltpu.CompilerParams(vmem_limit_bytes=FUSED_LIMIT),
         cost_estimate=cost(0, 20 << 20),
         name="finish",
@@ -1028,17 +1078,18 @@
     out_grad,
 ):
     members = lax.axis_size("head")
+    vt = value_weight.T
     (
         xs, n1t, hid, slope, prob, valt, mgt, fterms, res_grad, residual, down_y, up_y, ow_y, upb,
         sums2,
     ) = front(
         seq_len, tokens, out_grad, norm1_gain, norm1_bias, norm2_gain, norm2_bias, up_bias, f1_bias,
-        f2_bias, value_weight, f1_weight, f2_weight, out_weight, up_weight, down_weight,
+        f2_bias, vt, f1_weight, f2_weight, out_weight, up_weight, down_weight,
     )
     (
         result, input_grad, ow_parts, down_parts, up_parts, f1_parts, f2_parts, val_parts, small,
     ) = back(
-        seq_len, upb, sums2, norm1_gain, down_bias, value_weight, hid, slope, prob, n1t, valt, mgt,
+        seq_len, upb, sums2, norm1_gain, down_bias, vt, hid, slope, prob, n1t, valt, mgt,
         f1_weight, f2_weight, xs, fterms, down_y, up_y, ow_y, residual, res_grad,
     )
     (
@@ -1062,8 +1113,8 @@
         gain2_g,
         bias2_g,
         up_piece,
-        upb_all.reshape(-1),
-        down_piece,
+        upb_all,
+        down_piece.T,
         downb_g,
     )
 

time: 225 us -> 210 us (0.933)
  Pallas kernels: 219 us -> 207 us
  local copies, waits for them, and re-layouts: 5.06 us -> 0 us
    pallas_call x1, Pallas kernels: 123 us -> 113 us  [back(): pl.pallas_call(back_kernel, out_shape=out_shape, in_specs=[smem] + [vmem]...]
    unnamed x2 -> x0, local copies, waits for them, and re-layouts: 3.75 us -> none
where the time goes in v2:
time: 210 us; the launch traced here: 208 us
  Pallas kernels  207 us (99%)
    pallas_call x1, Pallas kernels, back(): pl.pallas_call(back_kernel, out_shape=out_shape, in_specs=[smem] + [vmem]...  113 us
    pallas_call x1, Pallas kernels, front(): pl.pallas_call(front_kernel, out_shape=out_shape, in_specs=[smem] + [anyw...  88.7 us
    pallas_call x1, Pallas kernels, finish(): pl.pallas_call(finish_kernel, grid=(1,), out_shape=out_shape, in_specs=[k...  5.28 us

profile of v2, /device:TPU:0, one launch (start us, length us, event | category | flops | bytes accessed | tf_op | source)
XLA Modules:
  0.0 207.8 jit_solution(13081974857389858491)
XLA Ops:
  0.7 88.7 %front.1 = (bf16[4,512,768]{2,1,0:T(8,128)(2,1)}, bf16[4,768,512]{2,1,0:T(8,128)(2,1)}, bf16[4,3,512,768]{3,2,1,0:T(8,128)(2,1)}, bf16[4,3,512,768]{3,2,1,0:T(8,...) custom-call(s32[16]{0:T(128)} %refs_0_.3, ...), custom_call_target="tpu_custom_call" | custom-call | flops 26575110144 | bytes 62914560 | tf_op jit(solution)/shard_map/front/pallas_call | solution.py:586
  89.3 113.0 %back.1 = (f32[512,768]{1,0:T(8,128)}, f32[512,768]{1,0:T(8,128)}, bf16[4,96,384]{2,1,0:T(8,128)(2,1)}, bf16[4,96,768]{2,1,0:T(8,128)(2,1)}, bf16[4,96,768]{2,1,...) custom-call(s32[16]{0:T(128)} %refs_0_.3, ...), custom_call_target="tpu_custom_call" | custom-call | flops 31406948352 | bytes 62914560 | tf_op jit(solution)/shard_map/back/pallas_call | solution.py:976
  202.3 5.3 %finish.1 = (f32[512,768]{1,0:T(8,128)}, f32[512,768]{1,0:T(8,128)}, f32[12,768]{1,0:T(8,128)}, f32[12,512]{1,0:T(8,128)}, f32[3072]{0:T(1024)}, /*index=5*/f32[...) custom-call(f32[512,768]{1,0:T(8,128)} %get-tuple-element.71.refs_0_, ...), custom_call_target="tpu_custom_call" | custom-call | bytes 20971520 | tf_op jit(solution)/shard_map/finish/pallas_call | solution.py:1049

commit v3 on v2

--- a/solution.py
+++ b/solution.py
@@ -52,18 +52,19 @@
     return pl.CostEstimate(flops=2 * macs, bytes_accessed=bytes_accessed, transcendentals=0)
 
 
-def store_shards(both, acc):
+def store_shards(both, acc, lanes=slice(None), far_first=False):
     _, count, depth, _ = both.shape
     me = lax.axis_index("dp")
     for d in range(2 * count):
-        side = jnp.bitwise_xor(me % 2, d % 2)
+        parity = jnp.bitwise_xor(me % 2, d % 2)
         other = jnp.bitwise_xor(me // 2, d // 2)
         gray = jnp.bitwise_xor(other, other // 2)
-        place, size, bit = 0, count // 2, 1
-        while size:
-            place = place + gray // bit % 2 * size
-            size, bit = size // 2, bit * 2
-        both[side, place] = acc[d * depth : (d + 1) * depth].astype(BF16)
+        bits = [gray // 2**i % 2 for i in range(len(masks(count)))]
+        bits = bits + [parity] if far_first else [parity] + bits
+        place = 0
+        for bit in bits[1:]:
+            place = 2 * place + bit
+        both[bits[0], place] = acc[d * depth : (d + 1) * depth, lanes].astype(BF16)
 
 
 def shard_shape(width, lanes):
@@ -99,17 +100,18 @@
 
 
 class Shards:
-    def __init__(self, wires, keep, send, got, out, own_sem, load_sem):
+    def __init__(self, wires, keep, send, got, out, own_sem, load_sem, far_first=False):
         self.keep, self.got, self.out, self.load_sem = keep, got, out, load_sem
         self.count = keep.shape[0]
-        self.first = None if send is None else wires.remote(send, got, "dp", 1)
+        order = [2 * mask for mask in masks(self.count)]
+        order = order + [1] if far_first else [1] + order
+        self.first = None if send is None else wires.remote(send, got, "dp", order[0])
         self.steps = []
         size = self.count
-        for mask in masks(self.count):
+        for step in order[1:]:
             size //= 2
             part = pl.ds(size, size)
-            move = wires.remote(keep.at[part], out.at[part], "dp", 2 * mask)
-            self.steps.append((size, move))
+            self.steps.append((size, wires.remote(keep.at[part], out.at[part], "dp", step)))
         self.own = pltpu.make_async_copy(keep.at[0], out.at[0], own_sem)
 
     def start(self):
@@ -626,10 +628,11 @@
     me = lax.axis_index("head")
     turns = slabs * heads
     w = Wires(r.send, r.recv)
-    sems = iter(range(4 * heads + 8))
-
-    def shards(keep, send, got, out):
-        return Shards(w, keep, send, got, out, r.store.at[next(sems)], r.store.at[next(sems)])
+    sems = iter(range(6 * heads + 8))
+
+    def shards(keep, send, got, out, far_first=False):
+        own_sem, load_sem = r.store.at[next(sems)], r.store.at[next(sems)]
+        return Shards(w, keep, send, got, out, own_sem, load_sem, far_first)
 
     down_group = shards(r.dk, None, r.dgot, r.down_o)
     up_group = shards(r.uk, r.up.at[1], r.ugot, r.up_o)
@@ -639,8 +642,9 @@
     for h in range(heads):
         both = r.bboth.at[h]
         f2_group.append(shards(both.at[0], both.at[1], r.bgot.at[h], r.f2_o.at[h]))
-        both = r.aboth.at[h]
-        f1_group.append(shards(both.at[0], both.at[1], r.agot.at[h], r.f1_o.at[h]))
+        for i in range(2):
+            both = r.aboth.at[h, i]
+            f1_group.append(shards(both.at[0], both.at[1], r.agot.at[h, i], r.f1_o.at[h, i]))
     val_group = shards(r.vboth.at[0], r.vboth.at[1], r.vgot, r.val_o)
     fterm1 = w.remote(r.fterms.at[1], r.fnear1, "head", 1)
     fterm3 = w.remote(r.fterms.at[3], r.fnear3, "head", 1)
@@ -656,7 +660,7 @@
     small_x = [
         w.remote(small_last, r.small_o.at[j], "head", j) for j in range(1, slabs)
     ]
-    base = 4 * heads + 8
+    base = 6 * heads + 8
     own_low = pltpu.make_async_copy(r.olow, r.ow_o.at[0], r.store.at[base])
     own_small = pltpu.make_async_copy(small_last, r.small_o.at[0], r.store.at[base + 1])
 
@@ -749,10 +753,13 @@
             @pl.when(turn == slabs * k + slabs - 1)
             def _(k=k):
                 store_shards(r.bboth.at[k], r.acc2)
-                f2_group[k].start()
-                store_shards(r.aboth.at[k], r.acc1)
                 if k < heads - 1:
-                    f1_group[k].start()
+                    f2_group[k].start()
+                for i in range(2):
+                    span = width // 2
+                    store_shards(r.aboth.at[k, i], r.acc1, slice(i * span, (i + 1) * span))
+                    if k < heads - 1:
+                        f1_group[2 * k + i].start()
 
         @pl.when(turn == 1)
         def _():
@@ -760,39 +767,48 @@
             r.fb[...] = add_low(r.fb[...], r.fnear3[...])
             fcross.start()
 
-        @pl.when(turn == slabs - 1)
+        @pl.when(turn == 2)
         def _():
             down_group.third()
 
-        @pl.when(turn == slabs)
+        @pl.when(turn == 4)
         def _():
             for copy in loads[9:]:
                 copy.wait()
             up_group.second()
 
-        @pl.when(turn == slabs + 2)
+        @pl.when(turn == 6)
         def _():
             out_group.second()
+
+        @pl.when(turn == 7)
+        def _():
             up_group.third()
 
-        @pl.when(turn == 2 * slabs)
+        @pl.when(turn == 8)
+        def _():
+            f2_group[0].second()
+
+        @pl.when(turn == 9)
         def _():
             out_group.third()
-            f2_group[0].second()
-
-        @pl.when(turn == 2 * slabs + 2)
-        def _():
+
+        @pl.when(turn == 10)
+        def _():
+            f1_group[0].second()
+
+        @pl.when(turn == 11)
+        def _():
+            f2_group[0].third()
             out_group.finish()
             r.olow[...] = (r.oall[0].astype(F32) + r.oall[1].astype(F32)).astype(BF16)
             for move in out_heads:
                 move.start()
             own_low.start()
-            f2_group[0].third()
 
         return carry
 
     lax.fori_loop(0, turns, turn_step, 0)
-    f1_group[0].second()
     for copy in loads[6:8]:
         copy.wait()
     res_load = load(8, r.res, r.resv)
@@ -823,6 +839,8 @@
         @pl.when(i == 0)
         def _():
             term3.start()
+            f1_group[1].second()
+            f1_group[0].third()
 
         @pl.when(i == 1)
         def _():
@@ -830,21 +848,22 @@
             term3.wait_send()
             r.crossb[...] = add_low(r.terms[2], r.near3[...])
             cross.start()
+            f1_group[1].third()
 
         @pl.when(i == 2)
         def _():
             term1.start()
-            f1_group[0].third()
-
-        @pl.when(i == 3)
-        def _():
             f2_group[1].second()
 
         return carry
 
     lax.fori_loop(0, slabs, term_step, 0)
     small_steps[0].start()
-    f1_group[-1].start()
+    f2_group[2].start()
+    f1_group[4].start()
+    f1_group[5].start()
+    f1_group[2].second()
+    f2_group[1].third()
     total = mm_nt(r.n1tv[0], r.vgt[0])
     for j in range(1, slabs):
         total += mm_nt(r.n1tv[j], r.vgt[j])
@@ -862,8 +881,16 @@
     r.resv[...] += r.fb[...].astype(F32) + others + flat_row(r.downb)
     finals = [pltpu.make_async_copy(r.resv, r.result, r.store.at[base + 2])]
     finals[0].start()
-    f2_group[1].third()
-    f1_group[1].second()
+
+    def small_step(i):
+        small_steps[i].wait_recv()
+        r.small[i + 1] = r.small[i] + r.small_in[i]
+        for after in small_steps[i + 1 : i + 2] or small_x + [own_small]:
+            after.start()
+
+    f1_group[3].second()
+    f1_group[2].third()
+    small_step(0)
     term1.wait_recv()
     cross.wait_recv()
     grad = r.terms[0].astype(F32) + r.near1[...].astype(F32) + r.crossr[...].astype(F32)
@@ -871,17 +898,17 @@
     r.rgv[...] += norm_back(grad, scaled, inv_std, flat_row(r.gain1))
     finals.append(pltpu.make_async_copy(r.rgv, r.input, r.store.at[base + 3]))
     finals[1].start()
-    f1_group[1].third()
+    small_step(1)
+    f1_group[3].third()
     f2_group[2].second()
-    for i, move in enumerate(small_steps):
-        move.wait_recv()
-        r.small[i + 1] = r.small[i] + r.small_in[i]
-        for after in small_steps[i + 1 : i + 2] or small_x + [own_small]:
-            after.start()
+    for i in range(2, len(steps)):
+        small_step(i)
+    f1_group[4].second()
     f2_group[2].third()
-    f1_group[2].second()
+    f1_group[5].second()
+    f1_group[4].third()
     val_group.second()
-    f1_group[2].third()
+    f1_group[5].third()
     val_group.third()
     for group in [down_group, up_group] + f2_group + f1_group + [val_group]:
         group.finish()
@@ -916,7 +943,7 @@
         low(slabs, part, span),
         low(count, part, width),
         low(count, part, width),
-        low(heads, count, part, width),
+        low(heads, 2, count, part, span),
         low(heads, count, part, longest),
         low(count, part, depth),
         wide(slabs, small, width),
@@ -924,7 +951,7 @@
     vl = lambda *s: pltpu.VMEM(s, BF16)
     vf = lambda *s: pltpu.VMEM(s, F32)
     steps = len(masks(count)) + 1
-    moves = 2 * (slabs - 1) + (2 * heads + 5) * steps + 6
+    moves = 2 * (slabs - 1) + (3 * heads + 5) * steps + 6
     scratch = dict(
         n1tv=vl(slabs, width, rows),
         valtv=vl(slabs, depth, rows),
@@ -956,8 +983,8 @@
         dgot=vl(count // 2, part, width),
         uk=vl(count, part, width),
         ugot=vl(count, part, width),
-        aboth=vl(heads, 2, count, part, width),
-        agot=vl(heads, count, part, width),
+        aboth=vl(heads, 2, 2, count, part, span),
+        agot=vl(heads, 2, count, part, span),
         bboth=vl(heads, 2, count, part, longest),
         bgot=vl(heads, count, part, longest),
         vboth=vl(2, count, part, depth),
@@ -968,7 +995,7 @@
         recv=pltpu.SemaphoreType.DMA((moves,)),
         load=pltpu.SemaphoreType.DMA((13,)),
         fetch=pltpu.SemaphoreType.DMA((2, 3)),
-        store=pltpu.SemaphoreType.DMA((12 + 4 * heads,)),
+        store=pltpu.SemaphoreType.DMA((12 + 6 * heads,)),
     )
     smem = pl.BlockSpec(memory_space=pltpu.SMEM)
     anywhere = pl.BlockSpec(memory_space=pl.ANY)
@@ -1020,7 +1047,8 @@
     up_o[...] = total(up)
     val_o[...] = total(val)
     for h in range(heads):
-        f1_o[h] = total(f1.at[h])
+        for i in range(2):
+            f1_o[h, :, i * span : (i + 1) * span] = total(f1.at[h, i])
         f2_o[h] = total(f2.at[h])
 
 
@@ -1045,7 +1073,8 @@
     whole = lambda v: pl.BlockSpec(v.shape, lambda _: (0,) * v.ndim)
     pair = lambda v: pl.BlockSpec((2,) + v.shape[1:], lambda _: (0, 0, 0))
     heads_pair = lambda v: pl.BlockSpec((heads, 2) + v.shape[2:], lambda _: (0, 0, 0, 0))
-    kinds = [whole] * 3 + [pair] * 2 + [whole] + [heads_pair] * 2 + [pair]
+    halves = lambda v: pl.BlockSpec((heads, 2, 2) + v.shape[3:], lambda _: (0,) * 5)
+    kinds = [whole] * 3 + [pair] * 2 + [whole, halves, heads_pair, pair]
     return pl.pallas_call(
         finish_kernel,
         grid=(1,),

time: 210 us -> 203 us (0.967)
  Pallas kernels: 207 us -> 202 us
    pallas_call x1, Pallas kernels: 113 us -> 108 us  [back(): pl.pallas_call(back_kernel, out_shape=out_shape, in_specs=[smem] + [vmem]...]
where the time goes in v3:
time: 203 us; the launch traced here: 202 us
  Pallas kernels  202 us (100%)
    pallas_call x1, Pallas kernels, back(): pl.pallas_call(back_kernel, out_shape=out_shape, in_specs=[smem] + [vmem]...  108 us
    pallas_call x1, Pallas kernels, front(): pl.pallas_call(front_kernel, out_shape=out_shape, in_specs=[smem] + [anyw...  88.7 us
    pallas_call x1, Pallas kernels, finish(): pl.pallas_call(finish_kernel, grid=(1,), out_shape=out_shape, in_specs=[k...  5.28 us

profile of v3, /device:TPU:0, one launch (start us, length us, event | category | flops | bytes accessed | tf_op | source)
XLA Modules:
  0.0 202.4 jit_solution(7269922631937001654)
XLA Ops:
  0.7 88.7 %front.1 = (bf16[4,512,768]{2,1,0:T(8,128)(2,1)}, bf16[4,768,512]{2,1,0:T(8,128)(2,1)}, bf16[4,3,512,768]{3,2,1,0:T(8,128)(2,1)}, bf16[4,3,512,768]{3,2,1,0:T(8,...) custom-call(s32[16]{0:T(128)} %refs_0_.3, ...), custom_call_target="tpu_custom_call" | custom-call | flops 26575110144 | bytes 62914560 | tf_op jit(solution)/shard_map/front/pallas_call | solution.py:588
  89.3 107.6 %back.1 = (f32[512,768]{1,0:T(8,128)}, f32[512,768]{1,0:T(8,128)}, bf16[4,96,384]{2,1,0:T(8,128)(2,1)}, bf16[4,96,768]{2,1,0:T(8,128)(2,1)}, bf16[4,96,768]{2,1,...) custom-call(s32[16]{0:T(128)} %refs_0_.3, ...), custom_call_target="tpu_custom_call" | custom-call | flops 31406948352 | bytes 62914560 | tf_op jit(solution)/shard_map/back/pallas_call | solution.py:1003
  196.9 5.3 %finish.1 = (f32[512,768]{1,0:T(8,128)}, f32[512,768]{1,0:T(8,128)}, f32[12,768]{1,0:T(8,128)}, f32[12,512]{1,0:T(8,128)}, f32[3072]{0:T(1024)}, /*index=5*/f32[...) custom-call(f32[512,768]{1,0:T(8,128)} %get-tuple-element.71.refs_0_, ...), custom_call_target="tpu_custom_call" | custom-call | bytes 20971520 | tf_op jit(solution)/shard_map/finish/pallas_call | solution.py:1078

commit v4 on v3

--- a/solution.py
+++ b/solution.py
@@ -173,12 +173,12 @@
 )
 FRONT_OUT = (
     "xs_o", "n1t_o", "hid_o", "slope_o", "prob_o", "valt_o", "mgt_o", "f_o", "rg_o", "res_o",
-    "down_o", "up_o", "ow_o", "upb_sum", "sums",
+    "down_o", "up1_o", "up2_o", "ow_o", "upb_sum", "sums",
 )
 FRONT_SCRATCH = (
     "xs", "n1", "n1t", "big", "f2v", "hidb", "slopeb", "probb", "valt", "attt", "owv", "upv",
     "downv", "ogs", "n2s", "pug", "near1", "near3", "crossb", "crossr", "fterms", "res", "mgts",
-    "acc", "ohalf", "osent", "ogot", "dboth", "dgot", "uboth", "oboth", "send", "recv",
+    "acc", "ohalf", "osent", "ogot", "dboth", "dgot", "uboth", "ugot", "oboth", "send", "recv",
     "load", "spill", "store",
 )
 
@@ -214,6 +214,7 @@
 
     w = Wires(r.send, r.recv)
     down_first = w.remote(r.dboth.at[1], r.dgot, "dp", 1)
+    up_first = w.remote(r.uboth.at[0, 1], r.ugot, "dp", 1)
 
     def remote(src, dst, step):
         return w.remote(src, dst, "head", step)
@@ -231,8 +232,6 @@
         "x2": remote(r.x, r.xs.at[2], 2),
         "x3": remote(r.xs.at[2], r.xs.at[3], 1),
         "o1": remote(r.og, r.ogs.at[1], 1),
-        "o2": remote(r.og, r.ogs.at[2], 2),
-        "o3": remote(r.ogs.at[2], r.ogs.at[3], 1),
         "t1": remote(r.terms.at[1], r.near1, 1),
     }
     columns = remote(r.osent, r.ogot, 1)
@@ -245,6 +244,8 @@
         moves[f"g{j}"] = remote(r.mgt.at[share(j)], r.mgts.at[j], j)
     for c in range(2):
         part = cut(c)
+        moves[f"o2{c}"] = remote(r.og.at[part], r.ogs.at[2, part], 2)
+        moves[f"o3{c}"] = remote(r.ogs.at[2, part], r.ogs.at[3, part], 1)
         moves[f"t3{c}"] = remote(r.terms.at[3, part], r.near3.at[part], 1)
         moves[f"c{c}"] = remote(r.crossb.at[part], r.crossr.at[part], 2)
 
@@ -290,7 +291,7 @@
         def _():
             moves["x2"].wait_recv()
             moves["x3"].start()
-            moves["o2"].start()
+            moves["o20"].start()
             moves["o1"].start()
 
         @pl.when(j == 3)
@@ -358,6 +359,8 @@
             def _(k=k):
                 far[k].start()
                 near[k].start()
+                if k == slabs - 1:
+                    moves["o21"].start()
 
         return carry
 
@@ -369,6 +372,8 @@
     ]
     for copy in stores:
         copy.start()
+    moves["o20"].wait_recv()
+    moves["o30"].start()
     for k in (2, 3):
         near[k].wait_recv()
         onward[k].wait_recv()
@@ -392,30 +397,40 @@
         return carry
 
     lax.fori_loop(2, 4, residual_step, 0)
-    moves["o2"].wait_recv()
-    moves["o3"].start()
+
+    def send_cross(c):
+        part = cut(c)
+        moves[f"t3{c}"].wait_recv()
+        r.crossb[part] = add_low(r.terms[2, part], r.near3[part])
+        moves[f"c{c}"].start()
 
     def ffn_step(u, carry):
-        j = jnp.where(u < 4, 2 + u % 2, (u - 4) // 2)
-        c = jnp.where(u < 4, u // 2, u % 2)
+        j = jnp.where(u < 2, 2 + u, jnp.where(u < 6, (u - 2) // 2, u - 4))
+        c = jnp.where(u < 2, 0, jnp.where(u < 6, u % 2, 1))
 
         @pl.when(u == 1)
         def _():
-            moves["o3"].wait_recv()
-
-        @pl.when(u == 2)
-        def _():
+            moves["o30"].wait_recv()
             for k in (2, 3):
                 far[k].wait_recv()
                 onward[k ^ 2].start()
 
-        @pl.when(u == 4)
+        @pl.when(u == 2)
         def _():
             for k in (0, 1):
                 near[k].wait_recv()
                 onward[k].wait_recv()
             moves["o1"].wait_recv()
             lax.fori_loop(0, 2, residual_step, 0)
+
+        @pl.when(u == 6)
+        def _():
+            moves["o21"].wait_recv()
+            moves["o31"].start()
+
+        @pl.when(u == 7)
+        def _():
+            moves["o31"].wait_recv()
 
         part = pl.ds(pl.multiple_of(c * half, half), half)
         gated, slope = silu_and_slope(mm(r.n2s[j, part], r.upv[...]) + flat_row(r.upb))
@@ -426,26 +441,26 @@
         r.terms[j, part] = mm_nt(pug, r.upv[...]).astype(BF16)
         r.fterms[j, part] = mm(act, r.downv[...]).astype(BF16)
 
-        for c in range(2):
-
-            @pl.when(u == 2 * c + 1)
-            def _(c=c):
-                moves[f"t3{c}"].start()
-
-            @pl.when(u == 2 * c + 2)
-            def _(c=c):
-                moves[f"t3{c}"].wait_recv()
-                part = cut(c)
-                r.crossb[part] = add_low(r.terms[2, part], r.near3[part])
-                moves[f"c{c}"].start()
+        @pl.when(u == 1)
+        def _():
+            moves["t30"].start()
+
+        @pl.when(u == 2)
+        def _():
+            send_cross(0)
+
+        @pl.when(u == 5)
+        def _():
+            moves["t1"].start()
 
         @pl.when(u == 7)
         def _():
-            moves["t1"].start()
+            moves["t31"].start()
 
         return carry
 
     lax.fori_loop(0, 8, ffn_step, 0)
+    send_cross(1)
     flat = (slabs * rows, width)
     r.acc[...] = mm_tn(r.ogs[...].reshape(flat), r.big[0 : slabs * rows])
     store_shards(r.dboth, r.acc)
@@ -482,13 +497,16 @@
     columns.start()
     r.ohalf[...] = r.acc[:, mine]
     r.acc[...] = mm_tn(r.n2s[...].reshape(flat), r.pug[...].reshape(flat))
-    store_shards(r.uboth, r.acc)
+    for i in range(2):
+        store_shards(r.uboth.at[i], r.acc, slice(i * span, (i + 1) * span))
+        if i == 0:
+            up_first.start()
     r.upb_sum[...] = jnp.sum(r.pug[...].reshape(flat).astype(F32), 0, keepdims=True)
     columns.wait_recv()
     r.ohalf[...] += r.ogot[...].astype(F32)
     store_shards(r.oboth, r.ohalf)
     more = [
-        pltpu.make_async_copy(r.uboth, r.up_o, r.store.at[4]),
+        pltpu.make_async_copy(r.uboth.at[1], r.up2_o, r.store.at[4]),
         pltpu.make_async_copy(r.oboth, r.ow_o, r.store.at[7]),
     ]
     for copy in more:
@@ -501,6 +519,10 @@
     down_first.wait_recv()
     add_got(r.dboth.at[0], r.dgot)
     stores.append(pltpu.make_async_copy(r.dboth.at[0], r.down_o, r.store.at[9]))
+    stores[-1].start()
+    up_first.wait_recv()
+    add_got(r.uboth.at[0, 0], r.ugot)
+    stores.append(pltpu.make_async_copy(r.uboth.at[0, 0], r.up1_o, r.store.at[10]))
     stores[-1].start()
     for copy in stores:
         copy.wait()
@@ -538,7 +560,8 @@
         wide(rows, width),
         wide(rows, width),
         jax.ShapeDtypeStruct(dsh.shape[1:], BF16),
-        dsh,
+        jax.ShapeDtypeStruct(osh.shape[1:], BF16),
+        osh,
         osh,
         wide(1, units),
         wide(3, width),
@@ -576,13 +599,14 @@
         ogot=vl(width, width // 2),
         dboth=vl(*dsh.shape),
         dgot=vl(*dsh.shape[1:]),
-        uboth=vl(*dsh.shape),
+        uboth=vl(2, *osh.shape),
+        ugot=vl(*osh.shape[1:]),
         oboth=vl(*osh.shape),
-        send=pltpu.SemaphoreType.DMA((12 + 4 * slabs,)),
-        recv=pltpu.SemaphoreType.DMA((12 + 4 * slabs,)),
+        send=pltpu.SemaphoreType.DMA((15 + 4 * slabs,)),
+        recv=pltpu.SemaphoreType.DMA((15 + 4 * slabs,)),
         load=pltpu.SemaphoreType.DMA((5 + 2 * heads,)),
         spill=pltpu.SemaphoreType.DMA((2, 3)),
-        store=pltpu.SemaphoreType.DMA((10,)),
+        store=pltpu.SemaphoreType.DMA((11,)),
     )
     smem = pl.BlockSpec(memory_space=pltpu.SMEM)
     return pl.pallas_call(
@@ -603,13 +627,13 @@
 
 BACK_IN = (
     "lens", "upb_sum", "sums", "gain1", "downb", "vt", "hid", "slope", "prob", "n1t", "valt", "mgt",
-    "f1", "f2", "xs", "fterms", "down", "up", "ow", "res", "rg",
+    "f1", "f2", "xs", "fterms", "down", "up1", "up2", "ow", "res", "rg",
 )
 BACK_OUT = ("result", "input", "ow_o", "down_o", "up_o", "f1_o", "f2_o", "val_o", "small_o")
 BACK_SCRATCH = (
     "n1tv", "valtv", "mgtv", "vgt", "f1v", "f2v", "terms", "probb", "sg", "pog",
     "acc1", "acc2", "acc3", "xb", "near3", "near1", "crossr", "fb", "fnear3",
-    "fnear1", "fcrossr", "rgv", "dk", "dgot", "uk", "ugot", "ok", "ogot", "oall", "olow", "aboth",
+    "fnear1", "fcrossr", "rgv", "dk", "dgot", "uk", "ugot", "vk", "vhalf", "ok", "ogot", "oall", "olow", "aboth",
     "agot", "bboth", "bgot", "vboth", "vgot", "small", "small_in", "send",
     "recv", "load", "fetch", "store",
 )
@@ -628,14 +652,15 @@
     me = lax.axis_index("head")
     turns = slabs * heads
     w = Wires(r.send, r.recv)
-    sems = iter(range(6 * heads + 8))
+    sems = iter(range(6 * heads + 10))
 
     def shards(keep, send, got, out, far_first=False):
         own_sem, load_sem = r.store.at[next(sems)], r.store.at[next(sems)]
         return Shards(w, keep, send, got, out, own_sem, load_sem, far_first)
 
     down_group = shards(r.dk, None, r.dgot, r.down_o)
-    up_group = shards(r.uk, r.up.at[1], r.ugot, r.up_o)
+    up1_group = shards(r.vk, None, r.vhalf, r.up_o.at[0])
+    up2_group = shards(r.uk, r.up2.at[1], r.ugot, r.up_o.at[1])
     out_group = shards(r.ok, r.ow.at[1], r.ogot, r.oall)
     out_heads = [w.remote(r.olow, r.ow_o.at[j], "head", j) for j in range(1, slabs)]
     f1_group, f2_group = [], []
@@ -660,7 +685,7 @@
     small_x = [
         w.remote(small_last, r.small_o.at[j], "head", j) for j in range(1, slabs)
     ]
-    base = 6 * heads + 8
+    base = 6 * heads + 10
     own_low = pltpu.make_async_copy(r.olow, r.ow_o.at[0], r.store.at[base])
     own_small = pltpu.make_async_copy(small_last, r.small_o.at[0], r.store.at[base + 1])
 
@@ -677,7 +702,7 @@
         load(6, r.f1, r.f1v),
         load(7, r.xs.at[3], r.xb),
         load(9, r.rg, r.rgv),
-        load(10, r.up.at[0], r.uk),
+        load(10, r.up2.at[0], r.uk),
         load(11, r.ow.at[0], r.ok),
     ]
 
@@ -689,10 +714,11 @@
             pltpu.make_async_copy(r.hid.at[j, h], r.terms.at[slot], r.fetch.at[slot, 2]),
         ]
 
-    for copy in loads[:2] + fetches(0) + loads[2:]:
+    up1_load = load(13, r.up1, r.vk)
+    for copy in loads[:2] + fetches(0) + loads[2:] + [up1_load]:
         copy.start()
     greet(partners(True))
-    up_group.start()
+    up2_group.start()
     out_group.start()
     fterm3.start()
     fterm1.start()
@@ -702,6 +728,8 @@
     for copy in loads[:6]:
         copy.wait()
     down_group.second()
+    up1_load.wait()
+    up1_group.second()
 
     def turn_step(turn, carry):
         h, j, slot = turn // slabs, turn % slabs, turn % 2
@@ -769,42 +797,42 @@
 
         @pl.when(turn == 2)
         def _():
-            down_group.third()
-
-        @pl.when(turn == 4)
-        def _():
             for copy in loads[9:]:
                 copy.wait()
-            up_group.second()
+            down_group.third()
+            up2_group.second()
+
+        @pl.when(turn == 3)
+        def _():
+            up1_group.third()
+
+        @pl.when(turn == 4)
+        def _():
+            out_group.second()
+            up2_group.third()
 
         @pl.when(turn == 6)
         def _():
-            out_group.second()
-
-        @pl.when(turn == 7)
-        def _():
-            up_group.third()
+            out_group.third()
+            f2_group[0].second()
 
         @pl.when(turn == 8)
         def _():
-            f2_group[0].second()
+            f1_group[0].second()
+            f2_group[0].third()
 
         @pl.when(turn == 9)
         def _():
-            out_group.third()
-
-        @pl.when(turn == 10)
-        def _():
-            f1_group[0].second()
-
-        @pl.when(turn == 11)
-        def _():
-            f2_group[0].third()
             out_group.finish()
             r.olow[...] = (r.oall[0].astype(F32) + r.oall[1].astype(F32)).astype(BF16)
             for move in out_heads:
                 move.start()
             own_low.start()
+
+        @pl.when(turn == 10)
+        def _():
+            f1_group[1].second()
+            f1_group[0].third()
 
         return carry
 
@@ -839,8 +867,7 @@
         @pl.when(i == 0)
         def _():
             term3.start()
-            f1_group[1].second()
-            f1_group[0].third()
+            f1_group[1].third()
 
         @pl.when(i == 1)
         def _():
@@ -848,12 +875,13 @@
             term3.wait_send()
             r.crossb[...] = add_low(r.terms[2], r.near3[...])
             cross.start()
-            f1_group[1].third()
+            f2_group[1].second()
 
         @pl.when(i == 2)
         def _():
             term1.start()
-            f2_group[1].second()
+            f1_group[2].second()
+            f2_group[1].third()
 
         return carry
 
@@ -862,8 +890,8 @@
     f2_group[2].start()
     f1_group[4].start()
     f1_group[5].start()
-    f1_group[2].second()
-    f2_group[1].third()
+    f1_group[3].second()
+    f1_group[2].third()
     total = mm_nt(r.n1tv[0], r.vgt[0])
     for j in range(1, slabs):
         total += mm_nt(r.n1tv[j], r.vgt[j])
@@ -888,9 +916,8 @@
         for after in small_steps[i + 1 : i + 2] or small_x + [own_small]:
             after.start()
 
-    f1_group[3].second()
-    f1_group[2].third()
     small_step(0)
+    f1_group[3].third()
     term1.wait_recv()
     cross.wait_recv()
     grad = r.terms[0].astype(F32) + r.near1[...].astype(F32) + r.crossr[...].astype(F32)
@@ -899,7 +926,6 @@
     finals.append(pltpu.make_async_copy(r.rgv, r.input, r.store.at[base + 3]))
     finals[1].start()
     small_step(1)
-    f1_group[3].third()
     f2_group[2].second()
     for i in range(2, len(steps)):
         small_step(i)
@@ -910,7 +936,7 @@
     val_group.second()
     f1_group[5].third()
     val_group.third()
-    for group in [down_group, up_group] + f2_group + f1_group + [val_group]:
+    for group in [down_group, up1_group, up2_group] + f2_group + f1_group + [val_group]:
         group.finish()
     for move in out_heads + small_x:
         move.wait_recv()
@@ -930,7 +956,7 @@
 
 
 def back(*args):
-    hid, f2, vt, ow = args[6], args[13], args[5], args[18]
+    hid, f2, vt, ow = args[6], args[13], args[5], args[19]
     slabs, heads, rows, width = hid.shape
     longest = f2.shape[2]
     depth = vt.shape[0]
@@ -942,7 +968,7 @@
         wide(rows, width),
         low(slabs, part, span),
         low(count, part, width),
-        low(count, part, width),
+        low(2, count, part, span),
         low(heads, 2, count, part, span),
         low(heads, count, part, longest),
         low(count, part, depth),
@@ -951,7 +977,7 @@
     vl = lambda *s: pltpu.VMEM(s, BF16)
     vf = lambda *s: pltpu.VMEM(s, F32)
     steps = len(masks(count)) + 1
-    moves = 2 * (slabs - 1) + (3 * heads + 5) * steps + 6
+    moves = 2 * (slabs - 1) + (3 * heads + 6) * steps + 6
     scratch = dict(
         n1tv=vl(slabs, width, rows),
         valtv=vl(slabs, depth, rows),
@@ -981,8 +1007,10 @@
         olow=vl(part, span),
         dk=vl(count, part, width),
         dgot=vl(count // 2, part, width),
-        uk=vl(count, part, width),
-        ugot=vl(count, part, width),
+        uk=vl(count, part, span),
+        ugot=vl(count, part, span),
+        vk=vl(count, part, span),
+        vhalf=vl(count // 2, part, span),
         aboth=vl(heads, 2, 2, count, part, span),
         agot=vl(heads, 2, count, part, span),
         bboth=vl(heads, 2, count, part, longest),
@@ -993,9 +1021,9 @@
         small_in=vf(steps, small, width),
         send=pltpu.SemaphoreType.DMA((moves,)),
         recv=pltpu.SemaphoreType.DMA((moves,)),
-        load=pltpu.SemaphoreType.DMA((13,)),
+        load=pltpu.SemaphoreType.DMA((14,)),
         fetch=pltpu.SemaphoreType.DMA((2, 3)),
-        store=pltpu.SemaphoreType.DMA((12 + 6 * heads,)),
+        store=pltpu.SemaphoreType.DMA((14 + 6 * heads,)),
     )
     smem = pl.BlockSpec(memory_space=pltpu.SMEM)
     anywhere = pl.BlockSpec(memory_space=pl.ANY)
@@ -1003,7 +1031,7 @@
     return pl.pallas_call(
         back_kernel,
         out_shape=out_shape,
-        in_specs=[smem] + [vmem] * 5 + [anywhere] * 15,
+        in_specs=[smem] + [vmem] * 5 + [anywhere] * 16,
         out_specs=[anywhere] * len(out_shape),
         scratch_shapes=[scratch[n] for n in BACK_SCRATCH],
         compiler_params=pltpu.CompilerParams(
@@ -1044,7 +1072,8 @@
     ow_o[:, theirs] = sum(ow[j].astype(F32) for j in range(1, slabs, 2))
     total = lambda ref: ref[0].astype(F32) + ref[1].astype(F32)
     down_o[...] = total(down)
-    up_o[...] = total(up)
+    for i in range(2):
+        up_o[:, i * span : (i + 1) * span] = total(up.at[i])
     val_o[...] = total(val)
     for h in range(heads):
         for i in range(2):
@@ -1073,8 +1102,9 @@
     whole = lambda v: pl.BlockSpec(v.shape, lambda _: (0,) * v.ndim)
     pair = lambda v: pl.BlockSpec((2,) + v.shape[1:], lambda _: (0, 0, 0))
     heads_pair = lambda v: pl.BlockSpec((heads, 2) + v.shape[2:], lambda _: (0, 0, 0, 0))
+    sides = lambda v: pl.BlockSpec((2, 2) + v.shape[2:], lambda _: (0,) * 4)
     halves = lambda v: pl.BlockSpec((heads, 2, 2) + v.shape[3:], lambda _: (0,) * 5)
-    kinds = [whole] * 3 + [pair] * 2 + [whole, halves, heads_pair, pair]
+    kinds = [whole] * 3 + [pair, sides, whole, halves, heads_pair, pair]
     return pl.pallas_call(
         finish_kernel,
         grid=(1,),
@@ -1109,8 +1139,8 @@
     members = lax.axis_size("head")
     vt = value_weight.T
     (
-        xs, n1t, hid, slope, prob, valt, mgt, fterms, res_grad, residual, down_y, up_y, ow_y, upb,
-        sums2,
+        xs, n1t, hid, slope, prob, valt, mgt, fterms, res_grad, residual, down_y, up1_y, up2_y, ow_y,
+        upb, sums2,
     ) = front(
         seq_len, tokens, out_grad, norm1_gain, norm1_bias, norm2_gain, norm2_bias, up_bias, f1_bias,
         f2_bias, vt, f1_weight, f2_weight, out_weight, up_weight, down_weight,
@@ -1119,7 +1149,7 @@
         result, input_grad, ow_parts, down_parts, up_parts, f1_parts, f2_parts, val_parts, small,
     ) = back(
         seq_len, upb, sums2, norm1_gain, down_bias, vt, hid, slope, prob, n1t, valt, mgt,
-        f1_weight, f2_weight, xs, fterms, down_y, up_y, ow_y, residual, res_grad,
+        f1_weight, f2_weight, xs, fterms, down_y, up1_y, up2_y, ow_y, residual, res_grad,
     )
     (
         result, input_grad, f1b_all, f2b_all, upb_all, down_piece, up_piece, out_piece, f1_piece,

time: 203 us -> 199 us (0.980)
  Pallas kernels: 202 us -> 198 us
    pallas_call x1, Pallas kernels: 108 us -> 100 us  [back(): pl.pallas_call(back_kernel, out_shape=out_shape, in_specs=[smem] + [vmem]...]
    pallas_call x1, Pallas kernels: 88.7 us -> 92.9 us  [front(): pl.pallas_call(front_kernel, out_shape=out_shape, in_specs=[smem] + [anyw...]
where the time goes in v4:
time: 199 us
  Pallas kernels  198 us (99%)
    pallas_call x1, Pallas kernels, back(): pl.pallas_call(back_kernel, out_shape=out_shape, in_specs=[smem] + [vmem]...  100 us
    pallas_call x1, Pallas kernels, front(): pl.pallas_call(front_kernel, out_shape=out_shape, in_specs=[smem] + [anyw...  92.9 us
    pallas_call x1, Pallas kernels, finish(): pl.pallas_call(finish_kernel, grid=(1,), out_shape=out_shape, in_specs=[k...  5.28 us

profile of v4, /device:TPU:0, one launch (start us, length us, event | category | flops | bytes accessed | tf_op | source)
XLA Modules:
  0.0 199.0 jit_solution(3643060600477116383)
XLA Ops:
  0.7 92.9 %front.1 = (bf16[4,512,768]{2,1,0:T(8,128)(2,1)}, bf16[4,768,512]{2,1,0:T(8,128)(2,1)}, bf16[4,3,512,768]{3,2,1,0:T(8,128)(2,1)}, bf16[4,3,512,768]{3,2,1,0:T(8,...) custom-call(s32[16]{0:T(128)} %refs_0_.3, ...), custom_call_target="tpu_custom_call" | custom-call | flops 26575110144 | bytes 62914560 | tf_op jit(solution)/shard_map/front/pallas_call | solution.py:612
  93.5 100.0 %back.1 = (f32[512,768]{1,0:T(8,128)}, f32[512,768]{1,0:T(8,128)}, bf16[4,96,384]{2,1,0:T(8,128)(2,1)}, bf16[4,96,768]{2,1,0:T(8,128)(2,1)}, bf16[2,4,96,384]{3,...) custom-call(s32[16]{0:T(128)} %refs_0_.3, ...), custom_call_target="tpu_custom_call" | custom-call | flops 31406948352 | bytes 62914560 | tf_op jit(solution)/shard_map/back/pallas_call | solution.py:1031
  193.5 5.3 %finish.1 = (f32[512,768]{1,0:T(8,128)}, f32[512,768]{1,0:T(8,128)}, f32[12,768]{1,0:T(8,128)}, f32[12,512]{1,0:T(8,128)}, f32[3072]{0:T(1024)}, /*index=5*/f32[...) custom-call(f32[512,768]{1,0:T(8,128)} %get-tuple-element.73.refs_0_, ...), custom_call_target="tpu_custom_call" | custom-call | bytes 20971520 | tf_op jit(solution)/shard_map/finish/pallas_call | solution.py:1108

commit v5 on v4

--- a/solution.py
+++ b/solution.py
@@ -241,7 +241,9 @@
         far.append(remote(r.attt.at[j, my_rows], r.attt.at[j ^ 2, my_rows], 2))
         onward.append(remote(r.attt.at[j, share(2)], r.attt.at[j ^ 1, share(2)], 1))
     for j in range(1, slabs):
-        moves[f"g{j}"] = remote(r.mgt.at[share(j)], r.mgts.at[j], j)
+        for c in range(2):
+            part = cut(c)
+            moves[f"g{j}{c}"] = remote(r.mgt.at[share(j), part], r.mgts.at[j, :, part], j)
     for c in range(2):
         part = cut(c)
         moves[f"o2{c}"] = remote(r.og.at[part], r.ogs.at[2, part], 2)
@@ -471,23 +473,26 @@
     ]
     for copy in stores:
         copy.start()
-    cot = r.ogs[0].astype(F32)
-    r.sums[2:3] = jnp.sum(cot, 0, keepdims=True)
     moves["t1"].wait_recv()
-    moves["c0"].wait_recv()
-    moves["c1"].wait_recv()
-
-    grad = r.terms[0].astype(F32) + r.near1[...].astype(F32) + r.crossr[...].astype(F32)
-    scaled, inv_std = standardize(r.res[...])
-    res_grad = cot + norm_back(grad, scaled, inv_std, flat_row(r.gain2))
-    r.rg_o[...] = res_grad
-    r.low[...] = res_grad.astype(BF16)
-    r.sums[0:1] = jnp.sum(grad * scaled, 0, keepdims=True)
-    r.sums[1:2] = jnp.sum(grad, 0, keepdims=True)
-    r.mgt[...] = mm_nt(r.owv[...], r.low[...]).astype(BF16)
-    for j in (2, 3, 1):
-        moves[f"g{j}"].start()
-        r.mgts[0] = r.mgt[my_rows]
+
+    for c in range(2):
+        part = slice(c * half, (c + 1) * half)
+        moves[f"c{c}"].wait_recv()
+        cot = r.ogs[0, part].astype(F32)
+        grad = r.terms[0, part].astype(F32) + r.near1[part].astype(F32)
+        grad += r.crossr[part].astype(F32)
+        scaled, inv_std = standardize(r.res[part])
+        res_grad = cot + norm_back(grad, scaled, inv_std, flat_row(r.gain2))
+        r.rg_o[part] = res_grad
+        r.low[part] = res_grad.astype(BF16)
+        r.mgt[:, part] = mm_nt(r.owv[...], r.low[part]).astype(BF16)
+        for j in (2, 3, 1):
+            moves[f"g{j}{c}"].start()
+        r.mgts[0, :, part] = r.mgt[my_rows, part]
+        for i, value in enumerate((grad * scaled, grad, cot)):
+            total = jnp.sum(value, 0, keepdims=True)
+            r.sums[i : i + 1] = total if c == 0 else r.sums[i : i + 1] + total
+
     mixed = r.attt[0]
     r.acc[...] = mm(mixed, r.low[...])
     span = width // 2
@@ -513,7 +518,8 @@
         copy.start()
     stores += more
     for j in range(1, slabs):
-        moves[f"g{j}"].wait_recv()
+        for c in range(2):
+            moves[f"g{j}{c}"].wait_recv()
     stores.append(pltpu.make_async_copy(r.mgts, r.mgt_o, r.store.at[8]))
     stores[-1].start()
     down_first.wait_recv()
@@ -602,8 +608,8 @@
         uboth=vl(2, *osh.shape),
         ugot=vl(*osh.shape[1:]),
         oboth=vl(*osh.shape),
-        send=pltpu.SemaphoreType.DMA((15 + 4 * slabs,)),
-        recv=pltpu.SemaphoreType.DMA((15 + 4 * slabs,)),
+        send=pltpu.SemaphoreType.DMA((14 + 5 * slabs,)),
+        recv=pltpu.SemaphoreType.DMA((14 + 5 * slabs,)),
         load=pltpu.SemaphoreType.DMA((5 + 2 * heads,)),
         spill=pltpu.SemaphoreType.DMA((2, 3)),
         store=pltpu.SemaphoreType.DMA((11,)),
@@ -781,8 +787,7 @@
             @pl.when(turn == slabs * k + slabs - 1)
             def _(k=k):
                 store_shards(r.bboth.at[k], r.acc2)
-                if k < heads - 1:
-                    f2_group[k].start()
+                f2_group[k].start()
                 for i in range(2):
                     span = width // 2
                     store_shards(r.aboth.at[k, i], r.acc1, slice(i * span, (i + 1) * span))
@@ -887,7 +892,6 @@
 
     lax.fori_loop(0, slabs, term_step, 0)
     small_steps[0].start()
-    f2_group[2].start()
     f1_group[4].start()
     f1_group[5].start()
     f1_group[3].second()

time: 199 us -> 198 us (level)
  no operation moved by 1% of the time
where the time goes in v5:
time: 198 us
  Pallas kernels  197 us (99%)
    pallas_call x1, Pallas kernels, back(): pl.pallas_call(back_kernel, out_shape=out_shape, in_specs=[smem] + [vmem]...  99.4 us
    pallas_call x1, Pallas kernels, front(): pl.pallas_call(front_kernel, out_shape=out_shape, in_specs=[smem] + [anyw...  92.1 us
    pallas_call x1, Pallas kernels, finish(): pl.pallas_call(finish_kernel, grid=(1,), out_shape=out_shape, in_specs=[k...  5.28 us

profile of v5, /device:TPU:0, one launch (start us, length us, event | category | flops | bytes accessed | tf_op | source)
XLA Modules:
  0.0 197.7 jit_solution(4554930193360094706)
XLA Ops:
  0.7 92.1 %front.1 = (bf16[4,512,768]{2,1,0:T(8,128)(2,1)}, bf16[4,768,512]{2,1,0:T(8,128)(2,1)}, bf16[4,3,512,768]{3,2,1,0:T(8,128)(2,1)}, bf16[4,3,512,768]{3,2,1,0:T(8,...) custom-call(s32[16]{0:T(128)} %refs_0_.3, ...), custom_call_target="tpu_custom_call" | custom-call | flops 26575110144 | bytes 62914560 | tf_op jit(solution)/shard_map/front/pallas_call | solution.py:618
  92.8 99.4 %back.1 = (f32[512,768]{1,0:T(8,128)}, f32[512,768]{1,0:T(8,128)}, bf16[4,96,384]{2,1,0:T(8,128)(2,1)}, bf16[4,96,768]{2,1,0:T(8,128)(2,1)}, bf16[2,4,96,384]{3,...) custom-call(s32[16]{0:T(128)} %refs_0_.3, ...), custom_call_target="tpu_custom_call" | custom-call | flops 31406948352 | bytes 62914560 | tf_op jit(solution)/shard_map/back/pallas_call | solution.py:1035
  192.2 5.3 %finish.1 = (f32[512,768]{1,0:T(8,128)}, f32[512,768]{1,0:T(8,128)}, f32[12,768]{1,0:T(8,128)}, f32[12,512]{1,0:T(8,128)}, f32[3072]{0:T(1024)}, /*index=5*/f32[...) custom-call(f32[512,768]{1,0:T(8,128)} %get-tuple-element.73.refs_0_, ...), custom_call_target="tpu_custom_call" | custom-call | bytes 20971520 | tf_op jit(solution)/shard_map/finish/pallas_call | solution.py:1112
